TPU v7x, 32 devices: a whole 2x2x4 slice. The times are simulated.
32 devices in a mesh: groups: 2 (over y), tok: 8 (over z, core), head: 2 (over x), tile: 1.
Axes of the slice: x: 2, y: 2, z: 4, core: 2. Of those that a mesh axis runs over, the one named last changes fastest.
Arguments:
- queries: bfloat16 [3072, 1, 16, 320], P(('groups', 'tok'), 'tile', 'head'), parts along dimension 0, may hold values from -6 to 6
- keys: bfloat16 [3072, 1, 16, 320], P(('groups', 'tok'), 'tile', 'head'), parts along dimension 0, may hold values from -6 to 6
- values: bfloat16 [3072, 1, 16, 320], P(('groups', 'tok'), 'tile', 'head'), parts along dimension 0, may hold values from -6 to 6
- rates: float32 [1, 16, 3072], P('tile', 'head', ('groups', 'tok')), parts along dimension 2, may hold values from 0.0003 to 0.003
- fast_weights: bfloat16 [1, 16, 3, 320, 320], P('tile', 'head'), may hold values from -0.3125 to 0.3125
- norm_gain: float32 [1, 16, 320], P('tile', 'head'), may hold values from 0.5 to 1.5
- frame_order: int32 [16], P('groups'), parts along dimension 0, may hold values from 0 to 7, each once
- gate_input: bfloat16 [24, 16, 8, 5120], P(None, ('groups', 'head'), 'tok', 'tile'), parts along dimension 1, may hold values from -6 to 6
- conv_weights: float32 [3, 3, 5120], P(None, None, 'tile'), may hold values from -2.5 to 2.5
Outputs:
- output: bfloat16 [24, 16, 8, 5120], P(None, ('groups', 'head'), 'tok', 'tile'), parts along dimension 1
There are 2 independent parts, one for each index of `groups`. A program takes and returns all parts, laid end to end along the dimension named above; an argument that names none is the same for every part. Nothing has to cross between parts.
Inputs may be any that keep to these rules, and one draw needn't show every extreme that they name: frame_order names each of the 8 frames once.
All inputs are finite; a program needn't handle non-finite values.
Results may differ from a plain program's by a relative error of at most 0.011.
Values may be sent and summed in bfloat16 or wider, within the bound.
No kernel may reach another device: no remote copies, remote signals or barrier semaphores. Data moves between devices by JAX's collectives and lax.ppermute only.
A program may use at most 64 MiB of HBM per device.

v0:
```python
import functools

import jax
import jax.numpy as jnp
from jax import lax
from jax.experimental import pallas as pl
from jax.experimental.pallas import tpu as pltpu
from jax.sharding import PartitionSpec as P

epsilon = 1e-06
LANES = 128
VMEM_BYTES = 24 * 1024 * 1024


def split_lanes(source, scratch, rows, head_size):
    full = head_size // LANES
    tail = head_size - full * LANES
    wide = source.reshape(rows, head_size).astype(jnp.float32)
    for tile in range(full):
        scratch[tile] = wide[:, tile * LANES : (tile + 1) * LANES]
    scratch[full, :, 0:tail] = wide[:, full * LANES :]


def join_halves(first, second, tail):
    lane = lax.broadcasted_iota(jnp.int32, first[-1].shape, 1)
    middle = jnp.where(lane < tail, first[-1], pltpu.roll(second[-1], tail, 1))
    return first[:-1] + [middle] + second[:-1]


def part_halves(packed, head_size):
    full = head_size // LANES
    tail = head_size - full * LANES
    first = packed[:, :head_size]
    middle = packed[:, head_size : (full + 1) * LANES]
    second = jnp.concatenate([packed[:, (full + 1) * LANES :], middle], axis=1)
    return first, second


def partner_head(partner):
    return lax.axis_index("tok") ^ partner


def pack_pairs(head, rate_ref, key_tiles, value_tiles, out_ref, start, head_size):
    heads, tok_rows = rate_ref.shape
    half = tok_rows // 2
    full = head_size // LANES
    tail = head_size - full * LANES
    rate_row = -rate_ref[pl.ds(head, 1), :]
    rates = jnp.broadcast_to(rate_row, (LANES, tok_rows)).T
    for row, tiles in ((start, key_tiles), (start + half, value_tiles)):
        sides = []
        for side in range(2):
            parts = [
                tiles[tile, pl.ds(side * half * heads + head, half, stride=heads), :]
                for tile in range(full + 1)
            ]
            if tiles is value_tiles:
                rate = rates[side * half : (side + 1) * half]
                parts = [rate * part for part in parts]
            sides.append(parts)
        for tile, part in enumerate(join_halves(sides[0], sides[1], tail)):
            out_ref[row : row + half, tile * LANES : (tile + 1) * LANES] = part.astype(jnp.bfloat16)


def pack_query(head, heads, height, query_tiles, out_ref, start, head_size):
    tok_rows = query_tiles.shape[1] // heads
    half = tok_rows // 2
    width = tok_rows // height
    full = head_size // LANES
    tail = head_size - full * LANES
    sides = []
    for side in range(2):
        sides.append(
            [
                jnp.concatenate(
                    [
                        query_tiles[
                            tile, pl.ds(column * heads + head, height, stride=width * heads), :
                        ]
                        for column in range(side * width // 2, (side + 1) * width // 2)
                    ],
                    axis=0,
                )
                for tile in range(full + 1)
            ]
        )
    for tile, part in enumerate(join_halves(sides[0], sides[1], tail)):
        out_ref[start : start + half, tile * LANES : (tile + 1) * LANES] = part.astype(jnp.bfloat16)


def pack_mirror_kernel(key_ref, value_ref, rate_ref, *rest):
    outs, (key_tiles, value_tiles) = rest[:-2], rest[-2:]
    tok_rows, heads, head_size = key_ref.shape
    split_lanes(key_ref[...], key_tiles, tok_rows * heads, head_size)
    split_lanes(value_ref[...], value_tiles, tok_rows * heads, head_size)
    for partner, out_ref in enumerate(outs):
        head = partner_head(partner ^ (heads // 2))
        pack_pairs(head, rate_ref, key_tiles, value_tiles, out_ref, 0, head_size)


def pack_across_kernel(height, query_any, *rest):
    outs, (query_ref, query_tiles, sems) = rest[:-3], rest[-3:]
    tok_rows, heads, head_size = query_any.shape
    half = tok_rows // 2
    full = head_size // LANES
    pieces = sems.shape[0]
    rows = tok_rows // pieces
    copies = [
        pltpu.make_async_copy(
            query_any.at[pl.ds(piece * rows, rows)],
            query_ref.at[pl.ds(piece * rows, rows)],
            sems.at[piece],
        )
        for piece in range(pieces)
    ]
    for copy in copies:
        copy.start()
    for piece, copy in enumerate(copies):
        copy.wait()
        wide = query_ref[piece * rows : (piece + 1) * rows].reshape(rows * heads, head_size)
        wide = wide.astype(jnp.float32)
        place = slice(piece * rows * heads, (piece + 1) * rows * heads)
        for tile in range(full):
            query_tiles[tile, place] = wide[:, tile * LANES : (tile + 1) * LANES]
        query_tiles[full, place, 0 : head_size - full * LANES] = wide[:, full * LANES :]
    for partner in range(heads // 2):
        head = partner_head(partner ^ (heads // 2))
        start = partner % 2 * half
        pack_query(head, heads, height, query_tiles, outs[partner // 2], start, head_size)


def pack_near_kernel(height, unread, key_ref, value_ref, rate_ref, query_ref, *rest):
    outs, (key_tiles, value_tiles, query_tiles) = rest[unread:-3], rest[-3:]
    tok_rows, heads, head_size = key_ref.shape
    split_lanes(key_ref[...], key_tiles, tok_rows * heads, head_size)
    split_lanes(value_ref[...], value_tiles, tok_rows * heads, head_size)
    split_lanes(query_ref[...], query_tiles, tok_rows * heads, head_size)
    line = heads // 2
    for partner in range(line):
        head = partner_head(partner)
        pack_pairs(head, rate_ref, key_tiles, value_tiles, outs[partner], 0, head_size)
        pack_query(head, heads, height, query_tiles, outs[line + partner], 0, head_size)


def send_far(part, partner, other):
    blocks = lax.axis_size("head")
    count = lax.axis_size("tok") * blocks
    pairs = [(place, place ^ (partner * blocks + other)) for place in range(count)]
    return lax.ppermute(part, ("tok", "head"), pairs)


def relay(landed):
    return [part for one in landed for part in (one, send(one, 1))]


def send(part, partner):
    pairs = [(place, place ^ partner) for place in range(lax.axis_size("tok"))]
    return lax.ppermute(part, "tok", pairs)


def sigmoid(value):
    return 0.5 + 0.5 * jnp.tanh(0.5 * value)


def contract(first, second, dims):
    return lax.dot_general(first, second, (dims, ((), ())), preferred_element_type=jnp.float32)


NN = ((1,), (0,))
NT = ((1,), (1,))


def add_gradients(pair_refs, tok_rows, weight_ref, prior_ref, grad_ref):
    half = tok_rows // 2
    head_size = weight_ref.shape[-1]
    first_weight = weight_ref[0]
    third_weight = weight_ref[1]
    down_turned = weight_ref[2].astype(jnp.float32).T.astype(jnp.bfloat16)
    step = 2 if len(pair_refs) % 2 == 0 else 1
    for start in range(0, len(pair_refs), step):
        key_parts, target_parts = [], []
        for pair_ref in pair_refs[start : start + step]:
            key_parts.extend(part_halves(pair_ref[0:half, :], head_size))
            target_parts.extend(part_halves(pair_ref[half:tok_rows, :], head_size))
        key_rows = jnp.concatenate(key_parts, axis=0)
        target = jnp.concatenate(target_parts, axis=0)
        first_pre = contract(first_weight, key_rows, NT)
        third_pre = contract(third_weight, key_rows, NT)
        hidden_grad = contract(down_turned, target, NT)
        sigmoid_first = sigmoid(first_pre)
        activated = first_pre * sigmoid_first
        mixed = (activated * third_pre).astype(jnp.bfloat16)
        grad_first_in = (
            hidden_grad * third_pre * sigmoid_first * (1.0 + first_pre * (1.0 - sigmoid_first))
        ).astype(jnp.bfloat16)
        grad_third_in = (hidden_grad * activated).astype(jnp.bfloat16)
        grads = (
            contract(grad_first_in, key_rows, NN),
            contract(grad_third_in, key_rows, NN),
            contract(mixed, target, NN),
        )
        for index, grad in enumerate(grads):
            if start == 0 and prior_ref is None:
                grad_ref[index, :, 0:head_size] = grad
            elif start == 0:
                grad_ref[index, :, 0:head_size] = prior_ref[index, :, 0:head_size] + grad
            else:
                grad_ref[index, :, 0:head_size] += grad


def sum_kernel(count, tok_rows, prior, *refs):
    pair_refs, weight_ref, out_ref = refs[:count], refs[count], refs[-1]
    prior_ref = refs[count + 1] if prior else None
    add_gradients(pair_refs, tok_rows, weight_ref, prior_ref, out_ref)


def mirror_kernel(count, tok_rows, *refs):
    pair_refs, weight_ref, prior_ref = refs[:count], refs[count], refs[count + 1]
    out_ref, grad_ref = refs[-2:]
    head_size = weight_ref.shape[-1]
    full = head_size // LANES
    tail = head_size - full * LANES
    half = head_size // 2
    add_gradients(pair_refs, tok_rows, weight_ref, prior_ref, grad_ref)

    def tiles_of(index, rows):
        return [
            grad_ref[index, rows, tile * LANES : (tile + 1) * LANES] for tile in range(full + 1)
        ]

    both = join_halves(tiles_of(0, slice(0, head_size)), tiles_of(1, slice(0, head_size)), tail)
    down = join_halves(tiles_of(2, slice(0, half)), tiles_of(2, slice(half, head_size)), tail)
    for tile, (above, below) in enumerate(zip(both, down)):
        lanes = slice(tile * LANES, (tile + 1) * LANES)
        out_ref[0:head_size, lanes] = above.astype(jnp.bfloat16)
        out_ref[head_size : head_size + half, lanes] = below.astype(jnp.bfloat16)


def renorm(weight_ref, grad_ref, mirror_refs, out_ref):
    head_size = weight_ref.shape[-1]
    units = head_size // len(mirror_refs)
    firsts, thirds, downs = [], [], []
    for mirror_ref in mirror_refs:
        first, third = part_halves(mirror_ref[0:units, :], head_size)
        firsts.append(first)
        thirds.append(third)
        downs.extend(part_halves(mirror_ref[units:, :], head_size))
    first, third, down = (jnp.concatenate(parts, axis=0) for parts in (firsts, thirds, downs))
    for index, other in enumerate((first, third, down)):
        before = weight_ref[index].astype(jnp.float32)
        axis = 1
        if index == 2:
            before = before.T
            axis = 0
        grad = grad_ref[index, :, 0:head_size] + other.astype(jnp.float32)
        updated = before - grad
        scale_old = jnp.sqrt(jnp.mean(before * before, axis=axis, keepdims=True) + epsilon)
        scale_new = jnp.sqrt(jnp.mean(updated * updated, axis=axis, keepdims=True) + epsilon)
        out_ref[index] = (updated * (scale_old / scale_new)).astype(jnp.bfloat16)


def apply_shards(
    height, frames_here, parts, order_ref, weight_ref, gain_ref, tap_ref, grid_ref, turned_ref
):
    head_size = weight_ref.shape[-1]
    full = head_size // LANES
    width = grid_ref.shape[2]
    top = 8
    edge = jnp.zeros((top, LANES), jnp.float32)
    for place in range(len(parts)):
        for tile in range(full + 1):
            for column in range(width):
                grid_ref[place, tile, column, 0:top] = edge
                grid_ref[place, tile, column, top + height :] = edge
    gain = gain_ref[...]
    for place, (shard, queries) in enumerate(parts):
        rows = jnp.concatenate(part_halves(queries, head_size), axis=0)
        proj_first = contract(rows, weight_ref[0], NT)
        proj_third = contract(rows, weight_ref[1], NT)
        mixed = (proj_first * jax.nn.sigmoid(proj_first) * proj_third).astype(jnp.bfloat16)
        outputs = contract(mixed, weight_ref[2], NN)
        scale = lax.rsqrt(jnp.mean(outputs * outputs, axis=-1, keepdims=True) + epsilon)
        normed = (outputs * scale * gain).astype(jnp.bfloat16).astype(jnp.float32)
        frame = order_ref[shard]
        block = frame // frames_here
        slot = frame % frames_here
        for tile in range(full + 1):
            lanes = slice(tile * LANES, min((tile + 1) * LANES, head_size))
            for column in range(width):
                grid_ref[place, tile, column, top : top + height, 0 : lanes.stop - lanes.start] = (
                    normed[column * height : (column + 1) * height, lanes]
                )
            taps = [
                tap_ref[index : index + 1, tile * LANES : (tile + 1) * LANES] for index in range(9)
            ]
            loaded = {}
            for column in range(width):
                total = None
                for col_tap in range(3):
                    source = column + col_tap - 1
                    if not 0 <= source < width:
                        continue
                    if source not in loaded:
                        loaded[source] = [
                            grid_ref[place, tile, source, first : first + height, :]
                            for first in range(top - 1, top + 2)
                        ]
                    for row_tap in range(3):
                        term = taps[row_tap * 3 + col_tap] * loaded[source][row_tap]
                        total = term if total is None else total + term
                turned_ref[
                    block, column, tile, pl.ds(slot, height, stride=frames_here), :
                ] = total


def apply_first_kernel(height, frames_here, near, far, order_ref, *refs):
    near_refs, far_refs = refs[: len(near)], refs[len(near) : len(near) + len(far)]
    before_ref, grad_ref, mirror_ref, gain_ref, tap_ref, weight_ref, turned_ref, grid_ref = refs[-8:]
    half = near_refs[0].shape[0]
    parts = [(shard, ref[...]) for shard, ref in zip(near, near_refs)]
    for shard, ref in zip(far, far_refs):
        parts.append((shard, ref[shard % 2 * half : (shard % 2 + 1) * half, :]))
    renorm(before_ref, grad_ref, [mirror_ref], weight_ref)
    apply_shards(
        height, frames_here, parts, order_ref, weight_ref, gain_ref, tap_ref, grid_ref, turned_ref
    )


def apply_last_kernel(height, frames_here, late, order, order_ref, *refs):
    query_refs = refs[: len(late)]
    weight_ref, done_ref, gain_ref, tap_ref = refs[len(late) : len(late) + 4]
    out_refs, (grid_ref, turned_ref) = refs[len(late) + 4 : -2], refs[-2:]
    turned_ref[...] = done_ref[...]
    parts = [(shard, ref[...]) for shard, ref in zip(late, query_refs)]
    apply_shards(
        height, frames_here, parts, order_ref, weight_ref, gain_ref, tap_ref, grid_ref, turned_ref
    )
    shards = turned_ref.shape[1]
    full = turned_ref.shape[2] - 1
    tail = weight_ref.shape[-1] - full * LANES
    blocks = turned_ref.shape[0]
    side_rows = turned_ref.shape[3] // 2
    for partner in range(shards):
        column = partner_head(partner)
        for other in range(blocks):
            block = lax.axis_index("head") ^ other
            sides = [
                [
                    turned_ref[block, column, tile, side * side_rows : (side + 1) * side_rows, :]
                    for tile in range(full + 1)
                ]
                for side in range(2)
            ]
            start = partner % 2 * side_rows
            if partner < 2 and other == 0:
                target, start = out_refs[partner], 0
            else:
                target = out_refs[2 + order.index((partner // 2 * 2, other))]
            for tile, part in enumerate(join_halves(sides[0], sides[1], tail)):
                target[start : start + side_rows, tile * LANES : (tile + 1) * LANES] = (
                    part.astype(jnp.bfloat16)
                )


def gate_kernel(blocks, shards, places, *refs):
    conv_refs = refs[: 2 * len(places)]
    gate_ref, out_any, product_ref, sems = refs[2 * len(places)], *refs[-3:]
    height = gate_ref.shape[0]
    frames_here = gate_ref.shape[1]
    head_size = gate_ref.shape[2] // blocks // shards
    side_rows = height * frames_here // 2
    rows_here = height // 2
    own = lax.axis_index("tok")
    odd = own % 2
    copies = []
    for index, (partner, other) in enumerate(places):
        one_ref, two_ref = conv_refs[2 * index : 2 * index + 2]
        one = one_ref[0:side_rows, :].astype(jnp.float32)
        two = two_ref[two_ref.shape[0] - side_rows :, :].astype(jnp.float32)
        low = part_halves(jnp.where(odd == 1, two, one), head_size)
        high = part_halves(jnp.where(odd == 1, one, two), head_size)
        head = (lax.axis_index("head") ^ other) * shards + ((own - odd) ^ partner)
        lanes = pl.ds(pl.multiple_of(head * head_size, 2 * head_size), 2 * head_size)
        for side in range(2):
            rows = slice(side * rows_here, (side + 1) * rows_here)
            conv = jnp.concatenate([low[side], high[side]], axis=1)
            conv = conv.reshape(rows_here, frames_here, 2 * head_size)
            gate = gate_ref[rows, :, lanes].astype(jnp.float32)
            product_ref[index, rows] = (conv * (gate * sigmoid(gate))).astype(jnp.bfloat16)
        copy = pltpu.make_async_copy(
            product_ref.at[index], out_any.at[:, :, lanes], sems.at[index]
        )
        copy.start()
        copies.append(copy)
    for copy in copies:
        copy.wait()


def in_vmem(count):
    return [pl.BlockSpec(memory_space=pltpu.VMEM)] * count


def call(kernel, out, operands, scratch=(), specs=None, leave=True):
    specs = specs or in_vmem(len(operands))
    operands = [
        pltpu.with_memory_space_constraint(item, pltpu.VMEM)
        if spec.memory_space == pltpu.VMEM
        else item
        for item, spec in zip(operands, specs)
    ]
    place = pltpu.VMEM if leave else pl.ANY
    if leave:
        out = jax.tree.map(lambda item: pltpu.VMEM(item.shape, item.dtype), out)
    return pl.pallas_call(
        kernel,
        out_shape=out,
        in_specs=specs,
        out_specs=jax.tree.map(lambda _: pl.BlockSpec(memory_space=place), out),
        scratch_shapes=scratch,
        compiler_params=pltpu.CompilerParams(vmem_limit_bytes=VMEM_BYTES),
        cost_estimate=pl.CostEstimate(flops=0, bytes_accessed=0, transcendentals=0),
    )(*operands)


def after(part, *earlier):
    anywhere = pl.BlockSpec(memory_space=pl.ANY)
    return pl.pallas_call(
        lambda *refs: None,
        out_shape=jax.ShapeDtypeStruct(part.shape, part.dtype),
        in_specs=[anywhere] * (1 + len(earlier)),
        out_specs=anywhere,
        input_output_aliases={0: 0},
        compiler_params=pltpu.CompilerParams(vmem_limit_bytes=1024 * 1024),
        cost_estimate=pl.CostEstimate(flops=0, bytes_accessed=0, transcendentals=0),
    )(part, *earlier)


def by_heads(
    queries, keys, values, rates, fast_weights, norm_gain, frame_order, gate_input, conv_weights
):
    tok_rows = queries.shape[0]
    head_count = queries.shape[1] * queries.shape[2]
    head_size = queries.shape[3]
    height, frames_here = gate_input.shape[:2]
    shards = lax.axis_size("tok")
    blocks = lax.axis_size("head")
    half = tok_rows // 2
    wide = 2 * head_size
    tiles = head_size // LANES + 1
    own = lax.axis_index("tok")
    own_channel = lax.axis_index("head") * head_count + own

    def rows_of(array):
        return array.reshape(tok_rows, head_count, head_size)

    def own_of(array, place):
        return lax.dynamic_index_in_dim(array, place, 0, keepdims=False)

    line = shards // 2
    tile_scratch = pltpu.VMEM((tiles, tok_rows * head_count, LANES), jnp.float32)
    token_rates = rates.reshape(head_count, tok_rows)
    chips = line // 2

    one = jax.ShapeDtypeStruct((tok_rows, wide), jnp.bfloat16)
    mirrored = call(
        pack_mirror_kernel,
        [one] * line,
        (rows_of(keys), rows_of(values), token_rates),
        (tile_scratch, tile_scratch),
    )
    mirrored = [mirrored[0]] + [send(mirrored[k], k) for k in range(1, line)]
    across = call(
        functools.partial(pack_across_kernel, height),
        [one] * chips,
        (pltpu.with_memory_space_constraint(rows_of(queries), pltpu.HBM),),
        (
            pltpu.VMEM((tok_rows, head_count, head_size), jnp.bfloat16),
            tile_scratch,
            pltpu.SemaphoreType.DMA((4,)),
        ),
        specs=[pl.BlockSpec(memory_space=pltpu.HBM)],
    )
    across_landed = [send(part, line + 2 * index) for index, part in enumerate(across)]
    weights = fast_weights.reshape(head_count, 3, head_size, head_size)
    own_weights = own_of(weights, own)
    mirror_weights = own_of(weights, own ^ line)
    own_gain = own_of(norm_gain.reshape(head_count, 1, head_size), own)
    taps = conv_weights.reshape(9, blocks * head_count, head_size)
    own_taps = lax.dynamic_index_in_dim(taps, own_channel, 1, keepdims=False)
    own_taps = jnp.pad(own_taps, ((0, 0), (0, tiles * LANES - head_size)))
    frames = frame_order[own ^ jnp.arange(shards, dtype=jnp.int32)]
    grad_shape = (3, head_size, tiles * LANES)
    grad_struct = jax.ShapeDtypeStruct(grad_shape, jnp.float32)
    unread = pl.BlockSpec(memory_space=pl.ANY)
    mirror_sum = call(
        functools.partial(sum_kernel, 2, tok_rows, False),
        grad_struct,
        (*mirrored[:2], mirror_weights),
    )
    early = (across[0], own_weights, own_gain, own_taps, frames, mirror_sum)
    query_struct = jax.ShapeDtypeStruct((half, wide), jnp.bfloat16)
    packed = call(
        functools.partial(pack_near_kernel, height, len(early)),
        [one] * line + [query_struct] * line,
        (rows_of(keys), rows_of(values), token_rates, rows_of(queries), *early),
        (tile_scratch, tile_scratch, tile_scratch),
        specs=in_vmem(4) + [unread] * len(early),
    )
    near_queries = packed[line:]
    held = [after(part, *mirrored[1:], *across_landed) for part in packed[1:line]]
    near = [packed[0]] + [send(held[k - 1], k) for k in range(1, line)]
    ahead = (*across_landed, *held)
    crossing = call(
        functools.partial(mirror_kernel, line - 2, tok_rows),
        jax.ShapeDtypeStruct((head_size + head_size // 2, wide), jnp.bfloat16),
        (*mirrored[2:], mirror_weights, mirror_sum, *ahead),
        (pltpu.VMEM(grad_shape, jnp.float32),),
        specs=in_vmem(line) + [unread] * len(ahead),
    )
    crossed = send(crossing, line)
    own_sum = call(
        functools.partial(sum_kernel, 2, tok_rows, False),
        grad_struct,
        (*near[:2], own_weights, crossing),
        specs=in_vmem(3) + [unread],
    )
    across = relay([after(part, own_sum) for part in across_landed])
    gradients = call(
        functools.partial(sum_kernel, line - 2, tok_rows, True),
        grad_struct,
        (*near[2:], own_weights, own_sum),
    )
    mate_queries = send(after(near_queries[1], own_sum), 1)
    late_queries = [
        send(after(near_queries[k], *near[2:]), k) for k in range(2, line)
    ]
    side_rows = frames_here * height // 2
    first_shards, far_shards, late_shards = (0, 1), range(line, shards), range(2, line)
    grid_shape = (tiles, shards, height + 16, LANES)
    turned_shape = (blocks, shards, tiles, 2 * side_rows, LANES)
    numbers = [pl.BlockSpec(memory_space=pltpu.SMEM)]
    updated, turned = call(
        functools.partial(apply_first_kernel, height, frames_here, first_shards, far_shards),
        [
            jax.ShapeDtypeStruct((3, head_size, head_size), jnp.bfloat16),
            jax.ShapeDtypeStruct(turned_shape, jnp.float32),
        ],
        (
            frames, near_queries[0], mate_queries, *across,
            own_weights, gradients, crossed, own_gain, own_taps,
        ),
        (pltpu.VMEM((2 + line, *grid_shape), jnp.float32),),
        specs=numbers + in_vmem(line + 7),
    )
    order = [(k, x) for k in range(0, shards, 2) for x in range(blocks)][1:]
    order = sorted(order, key=lambda place: (place != (line, 0), place))
    outgoing = call(
        functools.partial(apply_last_kernel, height, frames_here, late_shards, order),
        [jax.ShapeDtypeStruct((side_rows, wide), jnp.bfloat16)] * 2
        + [jax.ShapeDtypeStruct((2 * side_rows, wide), jnp.bfloat16)] * (shards // 2 * blocks - 1),
        (frames, *late_queries, updated, turned, own_gain, own_taps),
        (
            pltpu.VMEM((line - 2, *grid_shape), jnp.float32),
            pltpu.VMEM(turned_shape, jnp.float32),
        ),
        specs=numbers + in_vmem(line + 2),
    )
    landed = [send_far(part, k, x) for part, (k, x) in zip(outgoing[2:], order)]
    arrived = [outgoing[0], send(outgoing[1], 1), *relay(landed)]
    gate = gate_input.reshape(height, frames_here, gate_input.shape[3])
    places = [(0, 0), *order]
    gated = call(
        functools.partial(gate_kernel, blocks, shards, places),
        jax.ShapeDtypeStruct(gate.shape, jnp.bfloat16),
        (*arrived, gate),
        (
            pltpu.VMEM((len(places), *gate.shape[:2], wide), jnp.bfloat16),
            pltpu.SemaphoreType.DMA((len(places),)),
        ),
        leave=False,
    )
    return gated.reshape(gate_input.shape)


def fits_by_heads(queries, gate_input, frame_order):
    tok_rows, head_size = queries.shape[0], queries.shape[3]
    head_count = queries.shape[1] * queries.shape[2]
    height, frames_here, col_width = gate_input.shape[:3]
    shards = lax.axis_size("tok")
    return (
        head_count == shards
        and frame_order.shape[0] == shards
        and lax.axis_size("tile") == 1
        and col_width == 1
        and shards >= 8
        and shards & (shards - 1) == 0
        and head_size % LANES == LANES // 2
        and height % 8 == 0
        and tok_rows == height * shards
        and tok_rows % 64 == 0
        and head_size % 64 == 0
        and frames_here * height % 32 == 0
        and frames_here * lax.axis_size("head") == shards
        and lax.axis_size("head") & (lax.axis_size("head") - 1) == 0
    )


def renormed(previous, gradient):
    before = previous.astype(jnp.float32)
    updated = before - gradient
    scale_old = jnp.sqrt(jnp.mean(before * before, axis=-1, keepdims=True) + epsilon)
    scale_new = jnp.sqrt(jnp.mean(updated * updated, axis=-1, keepdims=True) + epsilon)
    return (updated * (scale_old / scale_new)).astype(jnp.bfloat16)


def by_tokens(
    queries, keys, values, rates, fast_weights, norm_gain, frame_order, gate_input, conv_weights
):
    tok_rows = queries.shape[0]
    head_count = queries.shape[1] * queries.shape[2]
    head_size = queries.shape[3]
    query_rows = queries.reshape(tok_rows, head_count, head_size)
    key_rows = keys.reshape(tok_rows, head_count, head_size)
    value_rows = values.reshape(tok_rows, head_count, head_size)
    token_rates = rates.reshape(head_count, tok_rows)
    weights = fast_weights.reshape(head_count, 3, head_size, head_size)
    head_gains = norm_gain.reshape(head_count, head_size)
    first_pre = jnp.einsum(
        "thd,hfd->htf", key_rows, weights[:, 0], preferred_element_type=jnp.float32
    )
    third_pre = jnp.einsum(
        "thd,hfd->htf", key_rows, weights[:, 1], preferred_element_type=jnp.float32
    )
    sigmoid_first = jax.nn.sigmoid(first_pre)
    activated = first_pre * sigmoid_first
    hidden = (activated * third_pre).astype(jnp.bfloat16)
    target = (-token_rates.T[:, :, None] * value_rows.astype(jnp.float32)).astype(jnp.bfloat16)
    grad_down = jnp.einsum("thd,htf->hdf", target, hidden, preferred_element_type=jnp.float32)
    hidden_grad = jnp.einsum(
        "thd,hdf->htf", target, weights[:, 2], preferred_element_type=jnp.float32
    )
    grad_first_in = (
        hidden_grad * third_pre * sigmoid_first * (1.0 + first_pre * (1.0 - sigmoid_first))
    ).astype(jnp.bfloat16)
    grad_third_in = (hidden_grad * activated).astype(jnp.bfloat16)
    grad_first = jnp.einsum(
        "htf,thd->hfd", grad_first_in, key_rows, preferred_element_type=jnp.float32
    )
    grad_third = jnp.einsum(
        "htf,thd->hfd", grad_third_in, key_rows, preferred_element_type=jnp.float32
    )
    gradients = jnp.stack([grad_first, grad_third, grad_down], axis=1)
    row_share = lax.psum_scatter(gradients, "tok", scatter_dimension=2, tiled=True)
    row_count = row_share.shape[2]
    own_rows = lax.dynamic_slice_in_dim(weights, lax.axis_index("tok") * row_count, row_count, 2)
    updated = lax.all_gather(renormed(own_rows, row_share), "tok", axis=2, tiled=True)
    proj_first = jnp.einsum(
        "thd,hfd->thf", query_rows, updated[:, 0], preferred_element_type=jnp.float32
    )
    proj_third = jnp.einsum(
        "thd,hfd->thf", query_rows, updated[:, 1], preferred_element_type=jnp.float32
    )
    mixed_hidden = (jax.nn.silu(proj_first) * proj_third).astype(jnp.bfloat16)
    outputs = jnp.einsum(
        "thf,hdf->thd", mixed_hidden, updated[:, 2], preferred_element_type=jnp.float32
    )
    normed = (
        outputs
        * lax.rsqrt(jnp.mean(outputs * outputs, axis=-1, keepdims=True) + epsilon)
        * head_gains[None]
    )
    normed = normed.astype(jnp.bfloat16)
    height = gate_input.shape[0]
    col_width = gate_input.shape[2]
    shards = lax.axis_size("tok")
    full_width = col_width * shards
    channels_here = head_count * head_size
    frame_grid = normed.reshape(height, full_width, channels_here)
    own_taps = lax.dynamic_slice_in_dim(
        conv_weights, lax.axis_index("head") * channels_here, channels_here, 2
    )
    padded = jnp.pad(frame_grid, ((1, 1), (1, 1), (0, 0)))
    local_sum = jnp.zeros((height, full_width, channels_here), jnp.float32)
    for row_tap in range(3):
        for col_tap in range(3):
            local_sum = local_sum + own_taps[row_tap, col_tap] * padded[
                row_tap : row_tap + height, col_tap : col_tap + full_width
            ].astype(jnp.float32)
    outgoing = local_sum.astype(jnp.bfloat16).reshape(height, shards, col_width, channels_here)
    arrived = lax.all_to_all(outgoing, "tok", split_axis=1, concat_axis=1, tiled=True)
    frame_count = frame_order.shape[0]
    numbers = jnp.arange(frame_count, dtype=jnp.int32)
    inverse = jnp.sum(
        jnp.where(frame_order[None, :] == numbers[:, None], numbers[None, :], 0), axis=1
    )
    ordered = jnp.take(arrived, inverse, axis=1)
    tile_block = lax.all_to_all(ordered, "head", split_axis=1, concat_axis=3, tiled=True)
    return (tile_block.astype(jnp.float32) * jax.nn.silu(gate_input.astype(jnp.float32))).astype(
        jnp.bfloat16
    )


def local(queries, keys, values, rates, fast_weights, norm_gain, frame_order, gate_input, conv_weights):
    args = (
        queries, keys, values, rates, fast_weights, norm_gain, frame_order, gate_input, conv_weights
    )
    if fits_by_heads(queries, gate_input, frame_order):
        return by_heads(*args)
    return by_tokens(*args)


def solution(mesh):
    in_specs = (
        P(("groups", "tok"), "tile", "head", None),
        P(("groups", "tok"), "tile", "head", None),
        P(("groups", "tok"), "tile", "head", None),
        P("tile", "head", ("groups", "tok")),
        P("tile", "head", None, None, None),
        P("tile", "head", None),
        P("groups"),
        P(None, ("groups", "head"), "tok", "tile"),
        P(None, None, "tile"),
    )
    out_specs = P(None, ("groups", "head"), "tok", "tile")
    return jax.shard_map(local, mesh=mesh, in_specs=in_specs, out_specs=out_specs, check_vma=False)
```

profile of v0, /device:TPU:13, one launch (start us, length us, event | category | flops | bytes accessed | tf_op | source)
XLA Modules:
  0.0 96.2 jit_solution(9947758501496346164)
XLA Ops:
  0.0 2.1 %shard_map.91 = (bf16[192,640]{1,0:T(8,128)(2,1)S(1)}, bf16[192,640]{1,0:T(8,128)(2,1)S(1)}) custom-call(bf16[192,8,320]{2,1,0:T(8,128)(2,1)} %bitcast.23), custom_call_target="tpu_custom_call" | custom-call | tf_op jit(solution)/shard_map/pallas_call | solution.py:414
  2.1 1.4 %collective-permute-start.4 = (bf16[192,640]{1,0:T(8,128)(2,1)S(1)}, bf16[192,640]{1,0:T(8,128)(2,1)S(1)}, u32[]{:S(2)}, u32[]{:S(2)}) collective-permute-start(bf16[192,640]{1,0:T(8,128)(2,1)S(1)} %get-tuple-element.37), channel_id=1, source_target_pairs={{0,12},{2,14},{4,8},{6,10},{8,4},{10,6},{12,0},{14,2},{1,13},{3,15... | collective-permute-start | bytes 737288 | tf_op jit(solution)/shard_map/ppermute | solution.py:158
  3.5 1.1 %collective-permute-start.3 = (bf16[192,640]{1,0:T(8,128)(2,1)S(1)}, bf16[192,640]{1,0:T(8,128)(2,1)S(1)}, u32[]{:S(2)}, u32[]{:S(2)}) collective-permute-start(bf16[192,640]{1,0:T(8,128)(2,1)S(1)} %get-tuple-element.30.rest_0_), channel_id=1, source_target_pairs={{0,8},{2,10},{4,12},{6,14},{8,0},{10,2},{12,4},{14,6},{1,9},{3,11}... | collective-permute-start | bytes 737288 | tf_op jit(solution)/shard_map/ppermute | solution.py:158
  4.6 1.3 %copy-done.2 = bf16[192,1,8,320]{3,2,1,0:T(8,128)(2,1)S(1)} copy-done((bf16[192,1,8,320]{3,2,1,0:T(8,128)(2,1)S(1)}, bf16[192,1,8,320]{3,2,1,0:T(8,128)(2,1)}, u32[]{:S(2)}) %copy-start.2) | copy-done | bytes 983064
  5.8 0.7 copy-done.6
  6.5 1.6 %shard_map.92 = (bf16[192,640]{1,0:T(8,128)(2,1)S(1)}, bf16[192,640]{1,0:T(8,128)(2,1)}, bf16[192,640]{1,0:T(8,128)(2,1)}, bf16[192,640]{1,0:T(8,128)(2,1)S(1)}) custom-call(bf16[192,8,320]{2,1,0:T(8,128)(2,1)S(1)} %bitcast.19, bf16[192,8,320]{2,1,0:T(8,128)(2,1)S(1)} %bitcast.21, f32[8,192]{1,0:T(8,128)S(1)} %bitcast.26), custom_call_target="tpu_custom_call" | custom-call | tf_op jit(solution)/shard_map/pallas_call | solution.py:414
  8.2 1.1 %collective-permute-start = (bf16[192,640]{1,0:T(8,128)(2,1)}, bf16[192,640]{1,0:T(8,128)(2,1)S(1)}, u32[]{:S(2)}, u32[]{:S(2)}) collective-permute-start(bf16[192,640]{1,0:T(8,128)(2,1)} %get-tuple-element.32), channel_id=1, source_target_pairs={{0,2},{2,0},{4,6},{6,4},{8,10},{10,8},{12,14},{14,12},{1,3},{3,1},... | collective-permute-start | bytes 737288 | tf_op jit(solution)/shard_map/ppermute | solution.py:158
  9.3 1.0 collective-permute-start.1
  10.2 0.7 collective-permute-start.2
  10.9 1.8 %reshape.52 = f32[9,16,320]{2,1,0:T(8,128)} reshape(f32[3,3,5120]{2,1,0:T(4,128)} %param.17) | data formatting | bytes 368640 | tf_op jit(solution)/shard_map/reshape | solution.py:488
  12.7 0.9 constant_dynamic-slice_fusion
  13.6 0.6 gather_fusion
  14.3 1.5 %dynamic-slice_bitcast_fusion = (bf16[3,320,320]{2,1,0:T(8,128)(2,1)S(1)}, bf16[3,320,320]{2,1,0:T(8,128)(2,1)S(1)}) fusion(bf16[1,8,3,320,320]{4,3,2,1,0:T(8,128)(2,1)} %param.13, s32[]{:T(128)S(6)} %select_n.26, s32[]{:T(128)S(6)} %select_n.24), kind=kLoop, calls=%fused_computation.1 | loop fusion | bytes 2457608 | tf_op jit(solution)/shard_map/jit(dynamic_index_in_dim)/squeeze | solution.py:457
  15.8 1.2 %shard_map.93.rest_5_.refs_3_ = f32[3,320,384]{2,1,0:T(8,128)S(1)} custom-call(bf16[192,640]{1,0:T(8,128)(2,1)S(1)} %get-tuple-element.31.refs_0_, bf16[192,640]{1,0:T(8,128)(2,1)S(1)} %collective-permute-done.refs_1_, bf16[3,320,320]{2,1,0:T(8,128)(2,1)S(1)} %get-tuple-element.55.refs_2_), custom_call_target="tpu_custom_call" | custom-call | tf_op jit(solution)/shard_map/pallas_call | solution.py:414
  17.4 1.8 %shard_map.94 = (bf16[192,640]{1,0:T(8,128)(2,1)S(1)}, bf16[192,640]{1,0:T(8,128)(2,1)S(1)}, bf16[192,640]{1,0:T(8,128)(2,1)S(1)}, bf16[192,640]{1,0:T(8,128)(2,...) custom-call(bf16[192,8,320]{2,1,0:T(8,128)(2,1)S(1)} %bitcast.20, ...), custom_call_target="tpu_custom_call" | custom-call | tf_op jit(solution)/shard_map/pallas_call | solution.py:414
  19.7 4.2 %collective-permute-done.3.refs_4_.refs_0_ = bf16[192,640]{1,0:T(8,128)(2,1)S(1)} collective-permute-done((bf16[192,640]{1,0:T(8,128)(2,1)S(1)}, bf16[192,640]{1,0:T(8,128)(2,1)S(1)}, u32[]{:S(2)}, u32[]{:S(2)}) %collective-permute-start.3) | collective-permute-done | bytes 245792 | tf_op jit(solution)/shard_map/ppermute | solution.py:158
  23.9 3.8 %collective-permute-done.2.refs_3_.refs_1_ = bf16[192,640]{1,0:T(8,128)(2,1)S(1)} collective-permute-done((bf16[192,640]{1,0:T(8,128)(2,1)S(1)}, bf16[192,640]{1,0:T(8,128)(2,1)S(1)}, u32[]{:S(2)}, u32[]{:S(2)}) %collective-permute-start.2) | collective-permute-done | bytes 245792 | tf_op jit(solution)/shard_map/ppermute | solution.py:158
  27.7 1.3 %shard_map.100.refs_3_ = bf16[480,640]{1,0:T(8,128)(2,1)S(1)} custom-call(bf16[192,640]{1,0:T(8,128)(2,1)S(1)} %collective-permute-done.1.refs_2_.refs_0_, bf16[192,640]{1,0:T(8,128)(2,1)S(1)} %collective-permute-done.2.refs_3_.refs_1_, bf16[3,320,320]{2,1,0:T(8,128)(2,1)S(1)} %get-tuple-element.55.refs_2_, f32[3,320,384]{2,1,0:T(8,128)S(1)} %shard_map.93.rest_5_.refs_3_, ...), custom_call_target="tpu_custom_call" | custom-call | tf_op jit(solution)/shard_map/pallas_call | solution.py:414
  29.0 2.9 %collective-permute-start.13 = (bf16[480,640]{1,0:T(8,128)(2,1)S(1)}, bf16[480,640]{1,0:T(8,128)(2,1)S(1)}, u32[]{:S(2)}, u32[]{:S(2)}) collective-permute-start(bf16[480,640]{1,0:T(8,128)(2,1)S(1)} %shard_map.100.refs_3_), channel_id=1, source_target_pairs={{0,8},{2,10},{4,12},{6,14},{8,0},{10,2},{12,4},{14,6},{1,9},{3,11}... | collective-permute-start | bytes 1843208 | tf_op jit(solution)/shard_map/ppermute | solution.py:158
  31.9 0.7 collective-permute-start.9
  32.6 1.4 %collective-permute-start.5 = (bf16[192,640]{1,0:T(8,128)(2,1)S(1)}, bf16[192,640]{1,0:T(8,128)(2,1)S(1)}, u32[]{:S(2)}, u32[]{:S(2)}) collective-permute-start(bf16[192,640]{1,0:T(8,128)(2,1)S(1)} %shard_map.95.refs_7_), channel_id=1, source_target_pairs={{0,4},{2,6},{4,0},{6,2},{8,12},{10,14},{12,8},{14,10},{1,5},{3,7},... | collective-permute-start | bytes 737288 | tf_op jit(solution)/shard_map/ppermute | solution.py:158
  34.0 1.2 %shard_map.101.refs_1_.refs_3_ = f32[3,320,384]{2,1,0:T(8,128)S(1)} custom-call(bf16[192,640]{1,0:T(8,128)(2,1)S(1)} %get-tuple-element.42.refs_0_, bf16[192,640]{1,0:T(8,128)(2,1)S(1)} %collective-permute-done.9.refs_1_, bf16[3,320,320]{2,1,0:T(8,128)(2,1)S(1)} %get-tuple-element.56.rest_1_.refs_2_.refs_6_, bf16[480,640]{1,0:T(8,128)(2,1)S(1)} %shard_map.100.refs_3_), custom_call_target="tpu_custom_call" | custom-call | tf_op jit(solution)/shard_map/pallas_call | solution.py:414
  35.2 0.8 collective-permute-start.11
  36.1 15.4 %collective-permute-done.6.refs_2_.refs_1_ = bf16[192,640]{1,0:T(8,128)(2,1)S(1)} collective-permute-done((bf16[192,640]{1,0:T(8,128)(2,1)S(1)}, bf16[192,640]{1,0:T(8,128)(2,1)S(1)}, u32[]{:S(2)}, u32[]{:S(2)}) %collective-permute-start.6) | collective-permute-done | bytes 245792 | tf_op jit(solution)/shard_map/ppermute | solution.py:158
  51.6 3.7 %collective-permute-done.5.refs_1_.refs_0_ = bf16[192,640]{1,0:T(8,128)(2,1)S(1)} collective-permute-done((bf16[192,640]{1,0:T(8,128)(2,1)S(1)}, bf16[192,640]{1,0:T(8,128)(2,1)S(1)}, u32[]{:S(2)}, u32[]{:S(2)}) %collective-permute-start.5) | collective-permute-done | bytes 245792 | tf_op jit(solution)/shard_map/ppermute | solution.py:158
  55.3 3.0 %collective-permute-start.8 = (bf16[96,640]{1,0:T(8,128)(2,1)S(1)}, bf16[96,640]{1,0:T(8,128)(2,1)S(1)}, u32[]{:S(2)}, u32[]{:S(2)}) collective-permute-start(bf16[96,640]{1,0:T(8,128)(2,1)S(1)} %shard_map.98), channel_id=1, source_target_pairs={{0,6},{2,4},{4,2},{6,0},{8,14},{10,12},{12,10},{14,8},{1,7},{3,5},... | collective-permute-start | bytes 368648 | tf_op jit(solution)/shard_map/ppermute | solution.py:158
  58.2 1.2 %shard_map.105.refs_7_ = f32[3,320,384]{2,1,0:T(8,128)S(1)} custom-call(bf16[192,640]{1,0:T(8,128)(2,1)S(1)} %collective-permute-done.5.refs_1_.refs_0_, bf16[192,640]{1,0:T(8,128)(2,1)S(1)} %collective-permute-done.6.refs_2_.refs_1_, bf16[3,320,320]{2,1,0:T(8,128)(2,1)S(1)} %get-tuple-element.56.rest_1_.refs_2_.refs_6_, ...), custom_call_target="tpu_custom_call" | custom-call | tf_op jit(solution)/shard_map/pallas_call | solution.py:414
  59.5 4.9 %shard_map.106 = (bf16[3,320,320]{2,1,0:T(8,128)(2,1)S(1)}, f32[2,8,3,96,128]{4,3,2,1,0:T(8,128)S(1)}) custom-call(s32[8]{0:T(128)S(1)} %gather_fusion, bf16[96,640]{1,0:T(8,128)(2,1)S(1)} %get-tuple-element.40.refs_0_, bf16[96,640]{1,0:T(8,128)(2,1)S(1)} %collective-permute-done.10.refs_1_, bf16[192,640]{1,0:T(8,128)(2,1)S(1)} %shard_map.103.refs_2_, ...), custom_call_target="tpu_custom_call" | custom-call | tf_op jit(solution)/shard_map/pallas_call | solution.py:414
  64.5 2.2 %shard_map.107 = (bf16[48,640]{1,0:T(8,128)(2,1)S(1)}, bf16[48,640]{1,0:T(8,128)(2,1)S(1)}, bf16[96,640]{1,0:T(8,128)(2,1)S(1)}, bf16[96,640]{1,0:T(8,128)(2,1)S...) custom-call(s32[8]{0:T(128)S(1)} %gather_fusion, ...), custom_call_target="tpu_custom_call" | custom-call | tf_op jit(solution)/shard_map/pallas_call | solution.py:414
  66.7 1.6 %collective-permute-start.15 = (bf16[96,640]{1,0:T(8,128)(2,1)S(1)}, bf16[96,640]{1,0:T(8,128)(2,1)S(1)}, u32[]{:S(2)}, u32[]{:S(2)}) collective-permute-start(bf16[96,640]{1,0:T(8,128)(2,1)S(1)} %get-tuple-element.48), channel_id=1, source_target_pairs={{0,8},{1,9},{2,10},{3,11},{4,12},{5,13},{6,14},{7,15},{8,0},{9,1},... | collective-permute-start | bytes 368648 | tf_op jit(solution)/shard_map/ppermute | solution.py:149
  68.3 1.2 %collective-permute-start.17 = (bf16[96,640]{1,0:T(8,128)(2,1)S(1)}, bf16[96,640]{1,0:T(8,128)(2,1)S(1)}, u32[]{:S(2)}, u32[]{:S(2)}) collective-permute-start(bf16[96,640]{1,0:T(8,128)(2,1)S(1)} %get-tuple-element.49), channel_id=1, source_target_pairs={{0,1},{1,0},{2,3},{3,2},{4,5},{5,4},{6,7},{7,6},{8,9},{9,8},{10,11... | collective-permute-start | bytes 368648 | tf_op jit(solution)/shard_map/ppermute | solution.py:149
  69.5 0.6 collective-permute-start.19
  70.2 0.8 collective-permute-start.21
  71.0 1.5 %collective-permute-start.14 = (bf16[48,640]{1,0:T(8,128)(2,1)S(1)}, bf16[48,640]{1,0:T(8,128)(2,1)S(1)}, u32[]{:S(2)}, u32[]{:S(2)}) collective-permute-start(bf16[48,640]{1,0:T(8,128)(2,1)S(1)} %get-tuple-element.47), channel_id=1, source_target_pairs={{0,2},{2,0},{4,6},{6,4},{8,10},{10,8},{12,14},{14,12},{1,3},{3,1},... | collective-permute-start | bytes 184328 | tf_op jit(solution)/shard_map/ppermute | solution.py:158
  72.5 0.9 collective-permute-done.14.refs_1_
  73.4 0.7 collective-permute-start.23
  74.1 1.1 %collective-permute-start.25 = (bf16[96,640]{1,0:T(8,128)(2,1)S(1)}, bf16[96,640]{1,0:T(8,128)(2,1)S(1)}, u32[]{:S(2)}, u32[]{:S(2)}) collective-permute-start(bf16[96,640]{1,0:T(8,128)(2,1)S(1)} %get-tuple-element.53), channel_id=1, source_target_pairs={{0,12},{1,13},{2,14},{3,15},{4,8},{5,9},{6,10},{7,11},{8,4},{9,5},... | collective-permute-start | bytes 368648 | tf_op jit(solution)/shard_map/ppermute | solution.py:149
  75.2 1.1 %collective-permute-start.27 = (bf16[96,640]{1,0:T(8,128)(2,1)S(1)}, bf16[96,640]{1,0:T(8,128)(2,1)S(1)}, u32[]{:S(2)}, u32[]{:S(2)}) collective-permute-start(bf16[96,640]{1,0:T(8,128)(2,1)S(1)} %get-tuple-element.54), channel_id=1, source_target_pairs={{0,13},{1,12},{2,15},{3,14},{4,9},{5,8},{6,11},{7,10},{8,5},{9,4},... | collective-permute-start | bytes 368648 | tf_op jit(solution)/shard_map/ppermute | solution.py:149
  76.3 1.7 %collective-permute-start.16 = (bf16[96,640]{1,0:T(8,128)(2,1)S(1)}, bf16[96,640]{1,0:T(8,128)(2,1)S(1)}, u32[]{:S(2)}, u32[]{:S(2)}) collective-permute-start(bf16[96,640]{1,0:T(8,128)(2,1)S(1)} %collective-permute-done.15.refs_2_), channel_id=1, source_target_pairs={{0,2},{2,0},{4,6},{6,4},{8,10},{10,8},{12,14},{14,12},{1,3},{3,1},... | collective-permute-start | bytes 368648 | tf_op jit(solution)/shard_map/ppermute | solution.py:158
  78.0 1.5 %collective-permute-done.21.refs_8_ = bf16[96,640]{1,0:T(8,128)(2,1)S(1)} collective-permute-done((bf16[96,640]{1,0:T(8,128)(2,1)S(1)}, bf16[96,640]{1,0:T(8,128)(2,1)S(1)}, u32[]{:S(2)}, u32[]{:S(2)}) %collective-permute-start.21) | collective-permute-done | bytes 122912 | tf_op jit(solution)/shard_map/ppermute | solution.py:149
  79.5 1.5 %collective-permute-start.18 = (bf16[96,640]{1,0:T(8,128)(2,1)S(1)}, bf16[96,640]{1,0:T(8,128)(2,1)S(1)}, u32[]{:S(2)}, u32[]{:S(2)}) collective-permute-start(bf16[96,640]{1,0:T(8,128)(2,1)S(1)} %collective-permute-done.17.refs_4_), channel_id=1, source_target_pairs={{0,2},{2,0},{4,6},{6,4},{8,10},{10,8},{12,14},{14,12},{1,3},{3,1},... | collective-permute-start | bytes 368648 | tf_op jit(solution)/shard_map/ppermute | solution.py:158
  81.0 0.6 collective-permute-done.23.refs_10_
  81.7 4.7 %collective-permute-start.20 = (bf16[96,640]{1,0:T(8,128)(2,1)S(1)}, bf16[96,640]{1,0:T(8,128)(2,1)S(1)}, u32[]{:S(2)}, u32[]{:S(2)}) collective-permute-start(bf16[96,640]{1,0:T(8,128)(2,1)S(1)} %collective-permute-done.19.refs_6_), channel_id=1, source_target_pairs={{0,2},{2,0},{4,6},{6,4},{8,10},{10,8},{12,14},{14,12},{1,3},{3,1},... | collective-permute-start | bytes 368648 | tf_op jit(solution)/shard_map/ppermute | solution.py:158
  86.3 2.6 %collective-permute-done.25.refs_12_ = bf16[96,640]{1,0:T(8,128)(2,1)S(1)} collective-permute-done((bf16[96,640]{1,0:T(8,128)(2,1)S(1)}, bf16[96,640]{1,0:T(8,128)(2,1)S(1)}, u32[]{:S(2)}, u32[]{:S(2)}) %collective-permute-start.25) | collective-permute-done | bytes 122912 | tf_op jit(solution)/shard_map/ppermute | solution.py:149
  88.9 2.0 %collective-permute-start.22 = (bf16[96,640]{1,0:T(8,128)(2,1)S(1)}, bf16[96,640]{1,0:T(8,128)(2,1)S(1)}, u32[]{:S(2)}, u32[]{:S(2)}) collective-permute-start(bf16[96,640]{1,0:T(8,128)(2,1)S(1)} %collective-permute-done.21.refs_8_), channel_id=1, source_target_pairs={{0,2},{2,0},{4,6},{6,4},{8,10},{10,8},{12,14},{14,12},{1,3},{3,1},... | collective-permute-start | bytes 368648 | tf_op jit(solution)/shard_map/ppermute | solution.py:158
  90.9 0.6 collective-permute-done.27.refs_14_
  91.5 1.2 %collective-permute-start.24 = (bf16[96,640]{1,0:T(8,128)(2,1)S(1)}, bf16[96,640]{1,0:T(8,128)(2,1)S(1)}, u32[]{:S(2)}, u32[]{:S(2)}) collective-permute-start(bf16[96,640]{1,0:T(8,128)(2,1)S(1)} %collective-permute-done.23.refs_10_), channel_id=1, source_target_pairs={{0,2},{2,0},{4,6},{6,4},{8,10},{10,8},{12,14},{14,12},{1,3},{3,1},... | collective-permute-start | bytes 368648 | tf_op jit(solution)/shard_map/ppermute | solution.py:158
  94.2 1.9 %shard_map.108 = bf16[24,4,5120]{2,1,0:T(4,128)(2,1)} custom-call(bf16[48,640]{1,0:T(8,128)(2,1)S(1)} %get-tuple-element.46.refs_0_, bf16[48,640]{1,0:T(8,128)(2,1)S(1)} %collective-permute-done.14.refs_1_, bf16[96,640]{1,0:T(8,128)(2,1)S(1)} %collective-permute-done.15.refs_2_, bf16[96,640]{1,0:T(8,128)(2,1)S(1)} %collective-permute-done.16.refs_3_, ...), custom_call_target="tpu_custom_call" | custom-call | tf_op jit(solution)/shard_map/pallas_call | solution.py:414
  (55 shorter events, 2.6 us)
Async XLA Ops:
  0.0 14.3 %copy-start = (f32[1,8,320]{2,1,0:T(8,128)S(1)}, f32[1,8,320]{2,1,0:T(8,128)}, u32[]{:S(2)}) copy-start(f32[1,8,320]{2,1,0:T(8,128)} %param.14) | copy-start | bytes 30724
  0.0 4.5 %copy-start.1 = (bf16[192,1,8,320]{3,2,1,0:T(8,128)(2,1)S(1)}, bf16[192,1,8,320]{3,2,1,0:T(8,128)(2,1)}, u32[]{:S(2)}) copy-start(bf16[192,1,8,320]{3,2,1,0:T(8,128)(2,1)} %param.10) | copy-start | bytes 2949124
  2.1 17.6 %collective-permute-start.4 = (bf16[192,640]{1,0:T(8,128)(2,1)S(1)}, bf16[192,640]{1,0:T(8,128)(2,1)S(1)}, u32[]{:S(2)}, u32[]{:S(2)}) collective-permute-start(bf16[192,640]{1,0:T(8,128)(2,1)S(1)} %get-tuple-element.37), channel_id=1, source_target_pairs={{0,12},{2,14},{4,8},{6,10},{8,4},{10,6},{12,0},{14,2},{1,13},{3,15... | collective-permute-start | bytes 737288 | tf_op jit(solution)/shard_map/ppermute | solution.py:158
  3.5 20.5 %collective-permute-start.3 = (bf16[192,640]{1,0:T(8,128)(2,1)S(1)}, bf16[192,640]{1,0:T(8,128)(2,1)S(1)}, u32[]{:S(2)}, u32[]{:S(2)}) collective-permute-start(bf16[192,640]{1,0:T(8,128)(2,1)S(1)} %get-tuple-element.30.rest_0_), channel_id=1, source_target_pairs={{0,8},{2,10},{4,12},{6,14},{8,0},{10,2},{12,4},{14,6},{1,9},{3,11}... | collective-permute-start | bytes 737288 | tf_op jit(solution)/shard_map/ppermute | solution.py:158
  4.6 1.3 %copy-start.2 = (bf16[192,1,8,320]{3,2,1,0:T(8,128)(2,1)S(1)}, bf16[192,1,8,320]{3,2,1,0:T(8,128)(2,1)}, u32[]{:S(2)}) copy-start(bf16[192,1,8,320]{3,2,1,0:T(8,128)(2,1)} %param.11) | copy-start | bytes 2949124
  5.8 0.7 copy-start.6
  6.5 7.1 %copy-start.8 = (s32[8]{0:T(128)S(1)}, s32[8]{0:T(128)}, u32[]{:S(2)}) copy-start(s32[8]{0:T(128)} %param.15) | copy-start | bytes 100
  8.2 7.7 %collective-permute-start = (bf16[192,640]{1,0:T(8,128)(2,1)}, bf16[192,640]{1,0:T(8,128)(2,1)S(1)}, u32[]{:S(2)}, u32[]{:S(2)}) collective-permute-start(bf16[192,640]{1,0:T(8,128)(2,1)} %get-tuple-element.32), channel_id=1, source_target_pairs={{0,2},{2,0},{4,6},{6,4},{8,10},{10,8},{12,14},{14,12},{1,3},{3,1},... | collective-permute-start | bytes 737288 | tf_op jit(solution)/shard_map/ppermute | solution.py:158
  9.3 14.7 %collective-permute-start.1 = (bf16[192,640]{1,0:T(8,128)(2,1)}, bf16[192,640]{1,0:T(8,128)(2,1)S(1)}, u32[]{:S(2)}, u32[]{:S(2)}) collective-permute-start(bf16[192,640]{1,0:T(8,128)(2,1)} %get-tuple-element.35), channel_id=1, source_target_pairs={{0,4},{2,6},{4,0},{6,2},{8,12},{10,14},{12,8},{14,10},{1,5},{3,7},... | collective-permute-start | bytes 737288 | tf_op jit(solution)/shard_map/ppermute | solution.py:158
  10.2 17.5 %collective-permute-start.2 = (bf16[192,640]{1,0:T(8,128)(2,1)S(1)}, bf16[192,640]{1,0:T(8,128)(2,1)S(1)}, u32[]{:S(2)}, u32[]{:S(2)}) collective-permute-start(bf16[192,640]{1,0:T(8,128)(2,1)S(1)} %get-tuple-element.36), channel_id=1, source_target_pairs={{0,6},{2,4},{4,2},{6,0},{8,14},{10,12},{12,10},{14,8},{1,7},{3,5},... | collective-permute-start | bytes 737288 | tf_op jit(solution)/shard_map/ppermute | solution.py:158
  15.8 1.3 %copy-start.3 = (bf16[192,1,8,320]{3,2,1,0:T(8,128)(2,1)S(1)}, bf16[192,1,8,320]{3,2,1,0:T(8,128)(2,1)}, u32[]{:S(2)}) copy-start(bf16[192,1,8,320]{3,2,1,0:T(8,128)(2,1)} %param.11) | copy-start | bytes 2949124
  15.8 1.6 %copy-start.4 = (bf16[192,1,8,320]{3,2,1,0:T(8,128)(2,1)S(1)}, bf16[192,1,8,320]{3,2,1,0:T(8,128)(2,1)}, u32[]{:S(2)}) copy-start(bf16[192,1,8,320]{3,2,1,0:T(8,128)(2,1)} %param.9) | copy-start | bytes 2949124
  15.8 1.6 %copy-start.7 = (f32[1,8,192]{2,1,0:T(8,128)S(1)}, f32[1,8,192]{2,1,0:T(8,128)}, u32[]{:S(2)}) copy-start(f32[1,8,192]{2,1,0:T(8,128)} %param.12) | copy-start | bytes 18436
  29.0 30.5 %collective-permute-start.13 = (bf16[480,640]{1,0:T(8,128)(2,1)S(1)}, bf16[480,640]{1,0:T(8,128)(2,1)S(1)}, u32[]{:S(2)}, u32[]{:S(2)}) collective-permute-start(bf16[480,640]{1,0:T(8,128)(2,1)S(1)} %shard_map.100.refs_3_), channel_id=1, source_target_pairs={{0,8},{2,10},{4,12},{6,14},{8,0},{10,2},{12,4},{14,6},{1,9},{3,11}... | collective-permute-start | bytes 1843208 | tf_op jit(solution)/shard_map/ppermute | solution.py:158
  31.9 2.0 %collective-permute-start.9 = (bf16[192,640]{1,0:T(8,128)(2,1)S(1)}, bf16[192,640]{1,0:T(8,128)(2,1)S(1)}, u32[]{:S(2)}, u32[]{:S(2)}) collective-permute-start(bf16[192,640]{1,0:T(8,128)(2,1)S(1)} %shard_map.99.refs_6_), channel_id=1, source_target_pairs={{0,2},{2,0},{4,6},{6,4},{8,10},{10,8},{12,14},{14,12},{1,3},{3,1},... | collective-permute-start | bytes 737288 | tf_op jit(solution)/shard_map/ppermute | solution.py:158
  32.6 18.9 %collective-permute-start.6 = (bf16[192,640]{1,0:T(8,128)(2,1)S(1)}, bf16[192,640]{1,0:T(8,128)(2,1)S(1)}, u32[]{:S(2)}, u32[]{:S(2)}) collective-permute-start(bf16[192,640]{1,0:T(8,128)(2,1)S(1)} %shard_map.96.refs_8_), channel_id=1, source_target_pairs={{0,6},{2,4},{4,2},{6,0},{8,14},{10,12},{12,10},{14,8},{1,7},{3,5},... | collective-permute-start | bytes 737288 | tf_op jit(solution)/shard_map/ppermute | solution.py:158
  32.6 22.6 %collective-permute-start.5 = (bf16[192,640]{1,0:T(8,128)(2,1)S(1)}, bf16[192,640]{1,0:T(8,128)(2,1)S(1)}, u32[]{:S(2)}, u32[]{:S(2)}) collective-permute-start(bf16[192,640]{1,0:T(8,128)(2,1)S(1)} %shard_map.95.refs_7_), channel_id=1, source_target_pairs={{0,4},{2,6},{4,0},{6,2},{8,12},{10,14},{12,8},{14,10},{1,5},{3,7},... | collective-permute-start | bytes 737288 | tf_op jit(solution)/shard_map/ppermute | solution.py:158
  35.2 24.2 %collective-permute-start.11 = (bf16[192,640]{1,0:T(8,128)(2,1)S(1)}, bf16[192,640]{1,0:T(8,128)(2,1)S(1)}, u32[]{:S(2)}, u32[]{:S(2)}) collective-permute-start(bf16[192,640]{1,0:T(8,128)(2,1)S(1)} %shard_map.103.refs_2_), channel_id=1, source_target_pairs={{0,2},{2,0},{4,6},{6,4},{8,10},{10,8},{12,14},{14,12},{1,3},{3,1},... | collective-permute-start | bytes 737288 | tf_op jit(solution)/shard_map/ppermute | solution.py:158
  36.1 23.4 %collective-permute-start.12 = (bf16[192,640]{1,0:T(8,128)(2,1)S(1)}, bf16[192,640]{1,0:T(8,128)(2,1)S(1)}, u32[]{:S(2)}, u32[]{:S(2)}) collective-permute-start(bf16[192,640]{1,0:T(8,128)(2,1)S(1)} %shard_map.104.refs_4_), channel_id=1, source_target_pairs={{0,2},{2,0},{4,6},{6,4},{8,10},{10,8},{12,14},{14,12},{1,3},{3,1},... | collective-permute-start | bytes 737288 | tf_op jit(solution)/shard_map/ppermute | solution.py:158
  51.6 3.7 %collective-permute-start.10 = (bf16[96,640]{1,0:T(8,128)(2,1)S(1)}, bf16[96,640]{1,0:T(8,128)(2,1)S(1)}, u32[]{:S(2)}, u32[]{:S(2)}) collective-permute-start(bf16[96,640]{1,0:T(8,128)(2,1)S(1)} %shard_map.102), channel_id=1, source_target_pairs={{0,2},{2,0},{4,6},{6,4},{8,10},{10,8},{12,14},{14,12},{1,3},{3,1},... | collective-permute-start | bytes 368648 | tf_op jit(solution)/shard_map/ppermute | solution.py:158
  55.2 9.2 %collective-permute-start.7 = (bf16[96,640]{1,0:T(8,128)(2,1)S(1)}, bf16[96,640]{1,0:T(8,128)(2,1)S(1)}, u32[]{:S(2)}, u32[]{:S(2)}) collective-permute-start(bf16[96,640]{1,0:T(8,128)(2,1)S(1)} %shard_map.97), channel_id=1, source_target_pairs={{0,4},{2,6},{4,0},{6,2},{8,12},{10,14},{12,8},{14,10},{1,5},{3,7},... | collective-permute-start | bytes 368648 | tf_op jit(solution)/shard_map/ppermute | solution.py:158
  55.3 9.2 %collective-permute-start.8 = (bf16[96,640]{1,0:T(8,128)(2,1)S(1)}, bf16[96,640]{1,0:T(8,128)(2,1)S(1)}, u32[]{:S(2)}, u32[]{:S(2)}) collective-permute-start(bf16[96,640]{1,0:T(8,128)(2,1)S(1)} %shard_map.98), channel_id=1, source_target_pairs={{0,6},{2,4},{4,2},{6,0},{8,14},{10,12},{12,10},{14,8},{1,7},{3,5},... | collective-permute-start | bytes 368648 | tf_op jit(solution)/shard_map/ppermute | solution.py:158
  64.4 29.7 %copy-start.5 = (bf16[24,4,1,5120]{3,1,2,0:T(4,128)(2,1)S(1)}, bf16[24,4,1,5120]{3,1,2,0:T(4,128)(2,1)}, u32[]{:S(2)}) copy-start(bf16[24,4,1,5120]{3,1,2,0:T(4,128)(2,1)} %param.16) | copy-start | bytes 2949124
  66.7 7.4 %collective-permute-start.15 = (bf16[96,640]{1,0:T(8,128)(2,1)S(1)}, bf16[96,640]{1,0:T(8,128)(2,1)S(1)}, u32[]{:S(2)}, u32[]{:S(2)}) collective-permute-start(bf16[96,640]{1,0:T(8,128)(2,1)S(1)} %get-tuple-element.48), channel_id=1, source_target_pairs={{0,8},{1,9},{2,10},{3,11},{4,12},{5,13},{6,14},{7,15},{8,0},{9,1},... | collective-permute-start | bytes 368648 | tf_op jit(solution)/shard_map/ppermute | solution.py:149
  68.3 6.9 %collective-permute-start.17 = (bf16[96,640]{1,0:T(8,128)(2,1)S(1)}, bf16[96,640]{1,0:T(8,128)(2,1)S(1)}, u32[]{:S(2)}, u32[]{:S(2)}) collective-permute-start(bf16[96,640]{1,0:T(8,128)(2,1)S(1)} %get-tuple-element.49), channel_id=1, source_target_pairs={{0,1},{1,0},{2,3},{3,2},{4,5},{5,4},{6,7},{7,6},{8,9},{9,8},{10,11... | collective-permute-start | bytes 368648 | tf_op jit(solution)/shard_map/ppermute | solution.py:149
  69.5 6.8 %collective-permute-start.19 = (bf16[96,640]{1,0:T(8,128)(2,1)S(1)}, bf16[96,640]{1,0:T(8,128)(2,1)S(1)}, u32[]{:S(2)}, u32[]{:S(2)}) collective-permute-start(bf16[96,640]{1,0:T(8,128)(2,1)S(1)} %get-tuple-element.50), channel_id=1, source_target_pairs={{0,4},{1,5},{2,6},{3,7},{4,0},{5,1},{6,2},{7,3},{8,12},{9,13},{10,... | collective-permute-start | bytes 368648 | tf_op jit(solution)/shard_map/ppermute | solution.py:149
  70.2 9.3 %collective-permute-start.21 = (bf16[96,640]{1,0:T(8,128)(2,1)S(1)}, bf16[96,640]{1,0:T(8,128)(2,1)S(1)}, u32[]{:S(2)}, u32[]{:S(2)}) collective-permute-start(bf16[96,640]{1,0:T(8,128)(2,1)S(1)} %get-tuple-element.51), channel_id=1, source_target_pairs={{0,5},{1,4},{2,7},{3,6},{4,1},{5,0},{6,3},{7,2},{8,13},{9,12},{10,... | collective-permute-start | bytes 368648 | tf_op jit(solution)/shard_map/ppermute | solution.py:149
  71.0 2.4 %collective-permute-start.14 = (bf16[48,640]{1,0:T(8,128)(2,1)S(1)}, bf16[48,640]{1,0:T(8,128)(2,1)S(1)}, u32[]{:S(2)}, u32[]{:S(2)}) collective-permute-start(bf16[48,640]{1,0:T(8,128)(2,1)S(1)} %get-tuple-element.47), channel_id=1, source_target_pairs={{0,2},{2,0},{4,6},{6,4},{8,10},{10,8},{12,14},{14,12},{1,3},{3,1},... | collective-permute-start | bytes 184328 | tf_op jit(solution)/shard_map/ppermute | solution.py:158
  73.4 8.3 %collective-permute-start.23 = (bf16[96,640]{1,0:T(8,128)(2,1)S(1)}, bf16[96,640]{1,0:T(8,128)(2,1)S(1)}, u32[]{:S(2)}, u32[]{:S(2)}) collective-permute-start(bf16[96,640]{1,0:T(8,128)(2,1)S(1)} %get-tuple-element.52), channel_id=1, source_target_pairs={{0,9},{1,8},{2,11},{3,10},{4,13},{5,12},{6,15},{7,14},{8,1},{9,0},... | collective-permute-start | bytes 368648 | tf_op jit(solution)/shard_map/ppermute | solution.py:149
  74.1 14.8 %collective-permute-start.25 = (bf16[96,640]{1,0:T(8,128)(2,1)S(1)}, bf16[96,640]{1,0:T(8,128)(2,1)S(1)}, u32[]{:S(2)}, u32[]{:S(2)}) collective-permute-start(bf16[96,640]{1,0:T(8,128)(2,1)S(1)} %get-tuple-element.53), channel_id=1, source_target_pairs={{0,12},{1,13},{2,14},{3,15},{4,8},{5,9},{6,10},{7,11},{8,4},{9,5},... | collective-permute-start | bytes 368648 | tf_op jit(solution)/shard_map/ppermute | solution.py:149
  75.2 16.2 %collective-permute-start.27 = (bf16[96,640]{1,0:T(8,128)(2,1)S(1)}, bf16[96,640]{1,0:T(8,128)(2,1)S(1)}, u32[]{:S(2)}, u32[]{:S(2)}) collective-permute-start(bf16[96,640]{1,0:T(8,128)(2,1)S(1)} %get-tuple-element.54), channel_id=1, source_target_pairs={{0,13},{1,12},{2,15},{3,14},{4,9},{5,8},{6,11},{7,10},{8,5},{9,4},... | collective-permute-start | bytes 368648 | tf_op jit(solution)/shard_map/ppermute | solution.py:149
  76.3 16.4 %collective-permute-start.16 = (bf16[96,640]{1,0:T(8,128)(2,1)S(1)}, bf16[96,640]{1,0:T(8,128)(2,1)S(1)}, u32[]{:S(2)}, u32[]{:S(2)}) collective-permute-start(bf16[96,640]{1,0:T(8,128)(2,1)S(1)} %collective-permute-done.15.refs_2_), channel_id=1, source_target_pairs={{0,2},{2,0},{4,6},{6,4},{8,10},{10,8},{12,14},{14,12},{1,3},{3,1},... | collective-permute-start | bytes 368648 | tf_op jit(solution)/shard_map/ppermute | solution.py:158
  79.5 13.2 %collective-permute-start.18 = (bf16[96,640]{1,0:T(8,128)(2,1)S(1)}, bf16[96,640]{1,0:T(8,128)(2,1)S(1)}, u32[]{:S(2)}, u32[]{:S(2)}) collective-permute-start(bf16[96,640]{1,0:T(8,128)(2,1)S(1)} %collective-permute-done.17.refs_4_), channel_id=1, source_target_pairs={{0,2},{2,0},{4,6},{6,4},{8,10},{10,8},{12,14},{14,12},{1,3},{3,1},... | collective-permute-start | bytes 368648 | tf_op jit(solution)/shard_map/ppermute | solution.py:158
  81.7 11.5 %collective-permute-start.20 = (bf16[96,640]{1,0:T(8,128)(2,1)S(1)}, bf16[96,640]{1,0:T(8,128)(2,1)S(1)}, u32[]{:S(2)}, u32[]{:S(2)}) collective-permute-start(bf16[96,640]{1,0:T(8,128)(2,1)S(1)} %collective-permute-done.19.refs_6_), channel_id=1, source_target_pairs={{0,2},{2,0},{4,6},{6,4},{8,10},{10,8},{12,14},{14,12},{1,3},{3,1},... | collective-permute-start | bytes 368648 | tf_op jit(solution)/shard_map/ppermute | solution.py:158
  88.9 4.2 %collective-permute-start.22 = (bf16[96,640]{1,0:T(8,128)(2,1)S(1)}, bf16[96,640]{1,0:T(8,128)(2,1)S(1)}, u32[]{:S(2)}, u32[]{:S(2)}) collective-permute-start(bf16[96,640]{1,0:T(8,128)(2,1)S(1)} %collective-permute-done.21.refs_8_), channel_id=1, source_target_pairs={{0,2},{2,0},{4,6},{6,4},{8,10},{10,8},{12,14},{14,12},{1,3},{3,1},... | collective-permute-start | bytes 368648 | tf_op jit(solution)/shard_map/ppermute | solution.py:158
  91.5 2.2 %collective-permute-start.24 = (bf16[96,640]{1,0:T(8,128)(2,1)S(1)}, bf16[96,640]{1,0:T(8,128)(2,1)S(1)}, u32[]{:S(2)}, u32[]{:S(2)}) collective-permute-start(bf16[96,640]{1,0:T(8,128)(2,1)S(1)} %collective-permute-done.23.refs_10_), channel_id=1, source_target_pairs={{0,2},{2,0},{4,6},{6,4},{8,10},{10,8},{12,14},{14,12},{1,3},{3,1},... | collective-permute-start | bytes 368648 | tf_op jit(solution)/shard_map/ppermute | solution.py:158
  92.7 1.3 %collective-permute-start.26 = (bf16[96,640]{1,0:T(8,128)(2,1)S(1)}, bf16[96,640]{1,0:T(8,128)(2,1)S(1)}, u32[]{:S(2)}, u32[]{:S(2)}) collective-permute-start(bf16[96,640]{1,0:T(8,128)(2,1)S(1)} %collective-permute-done.25.refs_12_), channel_id=1, source_target_pairs={{0,2},{2,0},{4,6},{6,4},{8,10},{10,8},{12,14},{14,12},{1,3},{3,1},... | collective-permute-start | bytes 368648 | tf_op jit(solution)/shard_map/ppermute | solution.py:158
  92.7 1.5 %collective-permute-start.28 = (bf16[96,640]{1,0:T(8,128)(2,1)S(1)}, bf16[96,640]{1,0:T(8,128)(2,1)S(1)}, u32[]{:S(2)}, u32[]{:S(2)}) collective-permute-start(bf16[96,640]{1,0:T(8,128)(2,1)S(1)} %collective-permute-done.27.refs_14_), channel_id=1, source_target_pairs={{0,2},{2,0},{4,6},{6,4},{8,10},{10,8},{12,14},{14,12},{1,3},{3,1},... | collective-permute-start | bytes 368648 | tf_op jit(solution)/shard_map/ppermute | solution.py:158
where the time goes:
time: 96.6 us; the launch traced here: 96.2 us
  waiting for transfers between devices  34.9 us (36%)
  starting transfers between devices  34.3 us (36%)
  Pallas kernels  19.5 us (20%)
  local copies, waits for them, and re-layouts  7.2 us (7%)
    ppermute x22, waiting for transfers between devices, send(): return lax.ppermute(part, 'tok', pairs)  29.5 us
    ppermute x22, starting transfers between devices, send(): return lax.ppermute(part, 'tok', pairs)  27.1 us
    pallas_call x10, Pallas kernels, call(): pl.pallas_call(kernel, out_shape=out, in_specs=specs, out_specs=jax.tree....  19.5 us
    ppermute x7, starting transfers between devices, send_far(): return lax.ppermute(part, ('tok', 'head'), pairs)  7.19 us
    ppermute x7, waiting for transfers between devices, send_far(): return lax.ppermute(part, ('tok', 'head'), pairs)  5.37 us
    unnamed x19, local copies, waits for them, and re-layouts  2.36 us
  transfers between devices with their start and end apart: 29, of which 13 were waited for; matrix products, arithmetic and copies ran while one was open for 5% of the time, Pallas kernels for 12%

commit v1 on v0

--- a/solution.py
+++ b/solution.py
@@ -362,12 +362,17 @@
                 )
 
 
+def silu_kernel(gate_ref, out_ref):
+    height, frames_here, channels = gate_ref.shape
+    gate = gate_ref[...].astype(jnp.float32)
+    out_ref[...] = (gate * jax.nn.sigmoid(gate)).reshape(height * frames_here, channels)
+
+
 def gate_kernel(blocks, shards, places, *refs):
     conv_refs = refs[: 2 * len(places)]
     gate_ref, out_any, product_ref, sems = refs[2 * len(places)], *refs[-3:]
-    height = gate_ref.shape[0]
-    frames_here = gate_ref.shape[1]
-    head_size = gate_ref.shape[2] // blocks // shards
+    height, frames_here, channels = out_any.shape
+    head_size = channels // blocks // shards
     side_rows = height * frames_here // 2
     rows_here = height // 2
     own = lax.axis_index("tok")
@@ -384,9 +389,9 @@
         for side in range(2):
             rows = slice(side * rows_here, (side + 1) * rows_here)
             conv = jnp.concatenate([low[side], high[side]], axis=1)
+            conv = conv * gate_ref[side * side_rows : (side + 1) * side_rows, lanes]
             conv = conv.reshape(rows_here, frames_here, 2 * head_size)
-            gate = gate_ref[rows, :, lanes].astype(jnp.float32)
-            product_ref[index, rows] = (conv * (gate * sigmoid(gate))).astype(jnp.bfloat16)
+            product_ref[index, rows] = conv.astype(jnp.bfloat16)
         copy = pltpu.make_async_copy(
             product_ref.at[index], out_any.at[:, :, lanes], sems.at[index]
         )
@@ -497,7 +502,13 @@
         grad_struct,
         (*mirrored[:2], mirror_weights),
     )
-    early = (across[0], own_weights, own_gain, own_taps, frames, mirror_sum)
+    gate = gate_input.reshape(height, frames_here, gate_input.shape[3])
+    opened = call(
+        silu_kernel,
+        jax.ShapeDtypeStruct((height * frames_here, gate_input.shape[3]), jnp.float32),
+        (gate,),
+    )
+    early = (opened, across[0], own_weights, own_gain, own_taps, frames, mirror_sum)
     query_struct = jax.ShapeDtypeStruct((half, wide), jnp.bfloat16)
     packed = call(
         functools.partial(pack_near_kernel, height, len(early)),
@@ -567,12 +578,11 @@
     )
     landed = [send_far(part, k, x) for part, (k, x) in zip(outgoing[2:], order)]
     arrived = [outgoing[0], send(outgoing[1], 1), *relay(landed)]
-    gate = gate_input.reshape(height, frames_here, gate_input.shape[3])
     places = [(0, 0), *order]
     gated = call(
         functools.partial(gate_kernel, blocks, shards, places),
         jax.ShapeDtypeStruct(gate.shape, jnp.bfloat16),
-        (*arrived, gate),
+        (*arrived, opened),
         (
             pltpu.VMEM((len(places), *gate.shape[:2], wide), jnp.bfloat16),
             pltpu.SemaphoreType.DMA((len(places),)),

time: 96.6 us -> 97.6 us (1.010)
  waiting for transfers between devices: 34.9 us -> 33.8 us
    unnamed x19 -> x25, local copies, waits for them, and re-layouts: 2.36 us -> 4.57 us
    pallas_call x10 -> x11, Pallas kernels: 19.5 us -> 20.3 us  [call(): pl.pallas_call(kernel, out_shape=out, in_specs=specs, out_specs=jax.tree....]
  transfers between devices with their start and end apart: 29 -> 29, of which waited for: 13 -> 12; matrix products, arithmetic and copies ran while one was open for 5% -> 3% of each run, Pallas kernels for 12% -> 13%
where the time goes in v1:
time: 97.6 us; the launch traced here: 97.2 us
  starting transfers between devices  34.7 us (36%)
  waiting for transfers between devices  33.8 us (35%)
  Pallas kernels  20.3 us (21%)
  local copies, waits for them, and re-layouts  7.93 us (8%)
    ppermute x22, waiting for transfers between devices, send(): return lax.ppermute(part, 'tok', pairs)  28.6 us
    ppermute x22, starting transfers between devices, send(): return lax.ppermute(part, 'tok', pairs)  27.5 us
    pallas_call x11, Pallas kernels, call(): pl.pallas_call(kernel, out_shape=out, in_specs=specs, out_specs=jax.tree....  20.3 us
    ppermute x7, starting transfers between devices, send_far(): return lax.ppermute(part, ('tok', 'head'), pairs)  7.21 us
    ppermute x7, waiting for transfers between devices, send_far(): return lax.ppermute(part, ('tok', 'head'), pairs)  5.16 us
    unnamed x25, local copies, waits for them, and re-layouts  4.57 us
  transfers between devices with their start and end apart: 29, of which 12 were waited for; matrix products, arithmetic and copies ran while one was open for 3% of the time, Pallas kernels for 13%

profile of v1, /device:TPU:13, one launch (start us, length us, event | category | flops | bytes accessed | tf_op | source)
XLA Modules:
  0.0 97.2 jit_solution(13440985282807476061)
XLA Ops:
  0.0 2.8 %shard_map.92 = (bf16[192,640]{1,0:T(8,128)(2,1)S(1)}, bf16[192,640]{1,0:T(8,128)(2,1)}) custom-call(bf16[192,8,320]{2,1,0:T(8,128)(2,1)} %bitcast.23), custom_call_target="tpu_custom_call" | custom-call | tf_op jit(solution)/shard_map/pallas_call | solution.py:419
  2.8 1.4 %collective-permute-start.4 = (bf16[192,640]{1,0:T(8,128)(2,1)}, bf16[192,640]{1,0:T(8,128)(2,1)S(1)}, u32[]{:S(2)}, u32[]{:S(2)}) collective-permute-start(bf16[192,640]{1,0:T(8,128)(2,1)} %get-tuple-element.37), channel_id=1, source_target_pairs={{0,12},{2,14},{4,8},{6,10},{8,4},{10,6},{12,0},{14,2},{1,13},{3,15... | collective-permute-start | bytes 737288 | tf_op jit(solution)/shard_map/ppermute | solution.py:158
  4.1 1.1 %collective-permute-start.3 = (bf16[192,640]{1,0:T(8,128)(2,1)S(1)}, bf16[192,640]{1,0:T(8,128)(2,1)S(1)}, u32[]{:S(2)}, u32[]{:S(2)}) collective-permute-start(bf16[192,640]{1,0:T(8,128)(2,1)S(1)} %get-tuple-element.30.rest_1_), channel_id=1, source_target_pairs={{0,8},{2,10},{4,12},{6,14},{8,0},{10,2},{12,4},{14,6},{1,9},{3,11}... | collective-permute-start | bytes 737288 | tf_op jit(solution)/shard_map/ppermute | solution.py:158
  5.2 1.3 %copy-done.3 = bf16[192,1,8,320]{3,2,1,0:T(8,128)(2,1)S(1)} copy-done((bf16[192,1,8,320]{3,2,1,0:T(8,128)(2,1)S(1)}, bf16[192,1,8,320]{3,2,1,0:T(8,128)(2,1)}, u32[]{:S(2)}) %copy-start.3) | copy-done | bytes 983064
  6.5 0.7 copy-done.9
  7.2 1.7 %shard_map.93 = (bf16[192,640]{1,0:T(8,128)(2,1)S(1)}, bf16[192,640]{1,0:T(8,128)(2,1)}, bf16[192,640]{1,0:T(8,128)(2,1)}, bf16[192,640]{1,0:T(8,128)(2,1)}) custom-call(bf16[192,8,320]{2,1,0:T(8,128)(2,1)S(1)} %bitcast.19, bf16[192,8,320]{2,1,0:T(8,128)(2,1)S(1)} %bitcast.21, f32[8,192]{1,0:T(8,128)S(1)} %bitcast.26), custom_call_target="tpu_custom_call" | custom-call | tf_op jit(solution)/shard_map/pallas_call | solution.py:419
  8.9 0.7 copy-done.7
  9.6 1.1 %collective-permute-start = (bf16[192,640]{1,0:T(8,128)(2,1)}, bf16[192,640]{1,0:T(8,128)(2,1)S(1)}, u32[]{:S(2)}, u32[]{:S(2)}) collective-permute-start(bf16[192,640]{1,0:T(8,128)(2,1)} %get-tuple-element.32), channel_id=1, source_target_pairs={{0,2},{2,0},{4,6},{6,4},{8,10},{10,8},{12,14},{14,12},{1,3},{3,1},... | collective-permute-start | bytes 737288 | tf_op jit(solution)/shard_map/ppermute | solution.py:158
  10.7 1.0 collective-permute-start.1
  11.6 0.7 collective-permute-start.2
  12.3 1.1 %reshape.53 = f32[9,16,320]{2,1,0:T(8,128)S(1)} reshape(f32[3,3,5120]{2,1,0:T(4,128)} %param.17) | data formatting | bytes 368640 | tf_op jit(solution)/shard_map/reshape | solution.py:493
  13.4 1.2 %copy-done.6 = bf16[24,4,1,5120]{3,1,2,0:T(4,128)(2,1)S(1)} copy-done((bf16[24,4,1,5120]{3,1,2,0:T(4,128)(2,1)S(1)}, bf16[24,4,1,5120]{3,1,2,0:T(4,128)(2,1)}, u32[]{:S(2)}) %copy-start.6) | copy-done | bytes 983064
  15.3 0.6 gather_fusion
  16.0 1.6 %dynamic-slice_bitcast_fusion = (bf16[3,320,320]{2,1,0:T(8,128)(2,1)S(1)}, bf16[3,320,320]{2,1,0:T(8,128)(2,1)S(1)}) fusion(bf16[1,8,3,320,320]{4,3,2,1,0:T(8,128)(2,1)} %param.13, s32[]{:T(128)S(6)} %select_n.26, s32[]{:T(128)S(6)} %select_n.24), kind=kLoop, calls=%fused_computation.1 | loop fusion | bytes 2457608 | tf_op jit(solution)/shard_map/jit(dynamic_index_in_dim)/squeeze | solution.py:462
  17.7 1.2 %shard_map.94.rest_6_.refs_3_ = f32[3,320,384]{2,1,0:T(8,128)S(1)} custom-call(bf16[192,640]{1,0:T(8,128)(2,1)S(1)} %copy-done.8, bf16[192,640]{1,0:T(8,128)(2,1)S(1)} %collective-permute-done.refs_1_, bf16[3,320,320]{2,1,0:T(8,128)(2,1)S(1)} %get-tuple-element.55.refs_2_), custom_call_target="tpu_custom_call" | custom-call | tf_op jit(solution)/shard_map/pallas_call | solution.py:419
  19.3 1.8 %shard_map.95 = (bf16[192,640]{1,0:T(8,128)(2,1)S(1)}, bf16[192,640]{1,0:T(8,128)(2,1)S(1)}, bf16[192,640]{1,0:T(8,128)(2,1)S(1)}, bf16[192,640]{1,0:T(8,128)(2,...) custom-call(bf16[192,8,320]{2,1,0:T(8,128)(2,1)S(1)} %bitcast.20, ...), custom_call_target="tpu_custom_call" | custom-call | tf_op jit(solution)/shard_map/pallas_call | solution.py:419
  21.1 3.8 %collective-permute-done.3.refs_4_.refs_0_ = bf16[192,640]{1,0:T(8,128)(2,1)S(1)} collective-permute-done((bf16[192,640]{1,0:T(8,128)(2,1)S(1)}, bf16[192,640]{1,0:T(8,128)(2,1)S(1)}, u32[]{:S(2)}, u32[]{:S(2)}) %collective-permute-start.3) | collective-permute-done | bytes 245792 | tf_op jit(solution)/shard_map/ppermute | solution.py:158
  24.8 3.8 %collective-permute-done.2.refs_3_.refs_1_ = bf16[192,640]{1,0:T(8,128)(2,1)S(1)} collective-permute-done((bf16[192,640]{1,0:T(8,128)(2,1)}, bf16[192,640]{1,0:T(8,128)(2,1)S(1)}, u32[]{:S(2)}, u32[]{:S(2)}) %collective-permute-start.2) | collective-permute-done | bytes 245792 | tf_op jit(solution)/shard_map/ppermute | solution.py:158
  28.6 1.3 %shard_map.101.refs_3_ = bf16[480,640]{1,0:T(8,128)(2,1)S(1)} custom-call(bf16[192,640]{1,0:T(8,128)(2,1)S(1)} %collective-permute-done.1.refs_2_.refs_0_, bf16[192,640]{1,0:T(8,128)(2,1)S(1)} %collective-permute-done.2.refs_3_.refs_1_, bf16[3,320,320]{2,1,0:T(8,128)(2,1)S(1)} %get-tuple-element.55.refs_2_, f32[3,320,384]{2,1,0:T(8,128)S(1)} %shard_map.94.rest_6_.refs_3_, ...), custom_call_target="tpu_custom_call" | custom-call | tf_op jit(solution)/shard_map/pallas_call | solution.py:419
  29.9 3.2 %collective-permute-start.13 = (bf16[480,640]{1,0:T(8,128)(2,1)S(1)}, bf16[480,640]{1,0:T(8,128)(2,1)S(1)}, u32[]{:S(2)}, u32[]{:S(2)}) collective-permute-start(bf16[480,640]{1,0:T(8,128)(2,1)S(1)} %shard_map.101.refs_3_), channel_id=1, source_target_pairs={{0,8},{2,10},{4,12},{6,14},{8,0},{10,2},{12,4},{14,6},{1,9},{3,11}... | collective-permute-start | bytes 1843208 | tf_op jit(solution)/shard_map/ppermute | solution.py:158
  33.1 0.7 collective-permute-start.9
  33.8 1.4 %collective-permute-start.5 = (bf16[192,640]{1,0:T(8,128)(2,1)S(1)}, bf16[192,640]{1,0:T(8,128)(2,1)S(1)}, u32[]{:S(2)}, u32[]{:S(2)}) collective-permute-start(bf16[192,640]{1,0:T(8,128)(2,1)S(1)} %shard_map.96.refs_7_), channel_id=1, source_target_pairs={{0,4},{2,6},{4,0},{6,2},{8,12},{10,14},{12,8},{14,10},{1,5},{3,7},... | collective-permute-start | bytes 737288 | tf_op jit(solution)/shard_map/ppermute | solution.py:158
  35.1 1.2 %shard_map.102.refs_1_.refs_3_ = f32[3,320,384]{2,1,0:T(8,128)S(1)} custom-call(bf16[192,640]{1,0:T(8,128)(2,1)S(1)} %get-tuple-element.42.refs_0_, bf16[192,640]{1,0:T(8,128)(2,1)S(1)} %collective-permute-done.9.refs_1_, bf16[3,320,320]{2,1,0:T(8,128)(2,1)S(1)} %get-tuple-element.56.rest_2_.refs_2_.refs_6_, bf16[480,640]{1,0:T(8,128)(2,1)S(1)} %shard_map.101.refs_3_), custom_call_target="tpu_custom_call" | custom-call | tf_op jit(solution)/shard_map/pallas_call | solution.py:419
  36.4 0.9 collective-permute-start.11
  37.3 15.5 %collective-permute-done.6.refs_2_.refs_1_ = bf16[192,640]{1,0:T(8,128)(2,1)S(1)} collective-permute-done((bf16[192,640]{1,0:T(8,128)(2,1)S(1)}, bf16[192,640]{1,0:T(8,128)(2,1)S(1)}, u32[]{:S(2)}, u32[]{:S(2)}) %collective-permute-start.6) | collective-permute-done | bytes 245792 | tf_op jit(solution)/shard_map/ppermute | solution.py:158
  52.8 3.7 %collective-permute-done.5.refs_1_.refs_0_ = bf16[192,640]{1,0:T(8,128)(2,1)S(1)} collective-permute-done((bf16[192,640]{1,0:T(8,128)(2,1)S(1)}, bf16[192,640]{1,0:T(8,128)(2,1)S(1)}, u32[]{:S(2)}, u32[]{:S(2)}) %collective-permute-start.5) | collective-permute-done | bytes 245792 | tf_op jit(solution)/shard_map/ppermute | solution.py:158
  56.5 3.0 %collective-permute-start.8 = (bf16[96,640]{1,0:T(8,128)(2,1)S(1)}, bf16[96,640]{1,0:T(8,128)(2,1)S(1)}, u32[]{:S(2)}, u32[]{:S(2)}) collective-permute-start(bf16[96,640]{1,0:T(8,128)(2,1)S(1)} %shard_map.99), channel_id=1, source_target_pairs={{0,6},{2,4},{4,2},{6,0},{8,14},{10,12},{12,10},{14,8},{1,7},{3,5},... | collective-permute-start | bytes 368648 | tf_op jit(solution)/shard_map/ppermute | solution.py:158
  59.5 1.3 %shard_map.106.refs_7_ = f32[3,320,384]{2,1,0:T(8,128)S(1)} custom-call(bf16[192,640]{1,0:T(8,128)(2,1)S(1)} %collective-permute-done.5.refs_1_.refs_0_, bf16[192,640]{1,0:T(8,128)(2,1)S(1)} %collective-permute-done.6.refs_2_.refs_1_, bf16[3,320,320]{2,1,0:T(8,128)(2,1)S(1)} %get-tuple-element.56.rest_2_.refs_2_.refs_6_, ...), custom_call_target="tpu_custom_call" | custom-call | tf_op jit(solution)/shard_map/pallas_call | solution.py:419
  60.8 4.9 %shard_map.107 = (bf16[3,320,320]{2,1,0:T(8,128)(2,1)S(1)}, f32[2,8,3,96,128]{4,3,2,1,0:T(8,128)S(1)}) custom-call(s32[8]{0:T(128)S(1)} %gather_fusion, bf16[96,640]{1,0:T(8,128)(2,1)S(1)} %get-tuple-element.40.refs_0_, bf16[96,640]{1,0:T(8,128)(2,1)S(1)} %collective-permute-done.10.refs_1_, bf16[192,640]{1,0:T(8,128)(2,1)S(1)} %shard_map.104.refs_2_, ...), custom_call_target="tpu_custom_call" | custom-call | tf_op jit(solution)/shard_map/pallas_call | solution.py:419
  65.8 2.3 %shard_map.108 = (bf16[48,640]{1,0:T(8,128)(2,1)S(1)}, bf16[48,640]{1,0:T(8,128)(2,1)S(1)}, bf16[96,640]{1,0:T(8,128)(2,1)S(1)}, bf16[96,640]{1,0:T(8,128)(2,1)S...) custom-call(s32[8]{0:T(128)S(1)} %gather_fusion, ...), custom_call_target="tpu_custom_call" | custom-call | tf_op jit(solution)/shard_map/pallas_call | solution.py:419
  68.1 1.6 %collective-permute-start.15 = (bf16[96,640]{1,0:T(8,128)(2,1)S(1)}, bf16[96,640]{1,0:T(8,128)(2,1)S(1)}, u32[]{:S(2)}, u32[]{:S(2)}) collective-permute-start(bf16[96,640]{1,0:T(8,128)(2,1)S(1)} %get-tuple-element.48), channel_id=1, source_target_pairs={{0,8},{1,9},{2,10},{3,11},{4,12},{5,13},{6,14},{7,15},{8,0},{9,1},... | collective-permute-start | bytes 368648 | tf_op jit(solution)/shard_map/ppermute | solution.py:149
  69.7 1.2 %collective-permute-start.17 = (bf16[96,640]{1,0:T(8,128)(2,1)S(1)}, bf16[96,640]{1,0:T(8,128)(2,1)S(1)}, u32[]{:S(2)}, u32[]{:S(2)}) collective-permute-start(bf16[96,640]{1,0:T(8,128)(2,1)S(1)} %get-tuple-element.49), channel_id=1, source_target_pairs={{0,1},{1,0},{2,3},{3,2},{4,5},{5,4},{6,7},{7,6},{8,9},{9,8},{10,11... | collective-permute-start | bytes 368648 | tf_op jit(solution)/shard_map/ppermute | solution.py:149
  71.5 0.9 collective-permute-start.21
  72.3 1.5 %collective-permute-start.14 = (bf16[48,640]{1,0:T(8,128)(2,1)S(1)}, bf16[48,640]{1,0:T(8,128)(2,1)S(1)}, u32[]{:S(2)}, u32[]{:S(2)}) collective-permute-start(bf16[48,640]{1,0:T(8,128)(2,1)S(1)} %get-tuple-element.47), channel_id=1, source_target_pairs={{0,2},{2,0},{4,6},{6,4},{8,10},{10,8},{12,14},{14,12},{1,3},{3,1},... | collective-permute-start | bytes 184328 | tf_op jit(solution)/shard_map/ppermute | solution.py:158
  73.8 0.9 collective-permute-done.14.refs_1_
  74.7 0.8 collective-permute-start.23
  75.5 1.1 %collective-permute-start.25 = (bf16[96,640]{1,0:T(8,128)(2,1)S(1)}, bf16[96,640]{1,0:T(8,128)(2,1)S(1)}, u32[]{:S(2)}, u32[]{:S(2)}) collective-permute-start(bf16[96,640]{1,0:T(8,128)(2,1)S(1)} %get-tuple-element.53), channel_id=1, source_target_pairs={{0,12},{1,13},{2,14},{3,15},{4,8},{5,9},{6,10},{7,11},{8,4},{9,5},... | collective-permute-start | bytes 368648 | tf_op jit(solution)/shard_map/ppermute | solution.py:149
  76.6 1.1 %collective-permute-start.27 = (bf16[96,640]{1,0:T(8,128)(2,1)S(1)}, bf16[96,640]{1,0:T(8,128)(2,1)S(1)}, u32[]{:S(2)}, u32[]{:S(2)}) collective-permute-start(bf16[96,640]{1,0:T(8,128)(2,1)S(1)} %get-tuple-element.54), channel_id=1, source_target_pairs={{0,13},{1,12},{2,15},{3,14},{4,9},{5,8},{6,11},{7,10},{8,5},{9,4},... | collective-permute-start | bytes 368648 | tf_op jit(solution)/shard_map/ppermute | solution.py:149
  77.7 1.7 %collective-permute-start.16 = (bf16[96,640]{1,0:T(8,128)(2,1)S(1)}, bf16[96,640]{1,0:T(8,128)(2,1)S(1)}, u32[]{:S(2)}, u32[]{:S(2)}) collective-permute-start(bf16[96,640]{1,0:T(8,128)(2,1)S(1)} %collective-permute-done.15.refs_2_), channel_id=1, source_target_pairs={{0,2},{2,0},{4,6},{6,4},{8,10},{10,8},{12,14},{14,12},{1,3},{3,1},... | collective-permute-start | bytes 368648 | tf_op jit(solution)/shard_map/ppermute | solution.py:158
  79.4 1.4 %collective-permute-done.21.refs_8_ = bf16[96,640]{1,0:T(8,128)(2,1)S(1)} collective-permute-done((bf16[96,640]{1,0:T(8,128)(2,1)S(1)}, bf16[96,640]{1,0:T(8,128)(2,1)S(1)}, u32[]{:S(2)}, u32[]{:S(2)}) %collective-permute-start.21) | collective-permute-done | bytes 122912 | tf_op jit(solution)/shard_map/ppermute | solution.py:149
  80.8 1.5 %collective-permute-start.18 = (bf16[96,640]{1,0:T(8,128)(2,1)S(1)}, bf16[96,640]{1,0:T(8,128)(2,1)S(1)}, u32[]{:S(2)}, u32[]{:S(2)}) collective-permute-start(bf16[96,640]{1,0:T(8,128)(2,1)S(1)} %collective-permute-done.17.refs_4_), channel_id=1, source_target_pairs={{0,2},{2,0},{4,6},{6,4},{8,10},{10,8},{12,14},{14,12},{1,3},{3,1},... | collective-permute-start | bytes 368648 | tf_op jit(solution)/shard_map/ppermute | solution.py:158
  82.3 0.7 collective-permute-done.23.refs_10_
  83.0 4.8 %collective-permute-start.20 = (bf16[96,640]{1,0:T(8,128)(2,1)S(1)}, bf16[96,640]{1,0:T(8,128)(2,1)S(1)}, u32[]{:S(2)}, u32[]{:S(2)}) collective-permute-start(bf16[96,640]{1,0:T(8,128)(2,1)S(1)} %collective-permute-done.19.refs_6_), channel_id=1, source_target_pairs={{0,2},{2,0},{4,6},{6,4},{8,10},{10,8},{12,14},{14,12},{1,3},{3,1},... | collective-permute-start | bytes 368648 | tf_op jit(solution)/shard_map/ppermute | solution.py:158
  87.8 2.5 %collective-permute-done.25.refs_12_ = bf16[96,640]{1,0:T(8,128)(2,1)S(1)} collective-permute-done((bf16[96,640]{1,0:T(8,128)(2,1)S(1)}, bf16[96,640]{1,0:T(8,128)(2,1)S(1)}, u32[]{:S(2)}, u32[]{:S(2)}) %collective-permute-start.25) | collective-permute-done | bytes 122912 | tf_op jit(solution)/shard_map/ppermute | solution.py:149
  90.3 2.0 %collective-permute-start.22 = (bf16[96,640]{1,0:T(8,128)(2,1)S(1)}, bf16[96,640]{1,0:T(8,128)(2,1)S(1)}, u32[]{:S(2)}, u32[]{:S(2)}) collective-permute-start(bf16[96,640]{1,0:T(8,128)(2,1)S(1)} %collective-permute-done.21.refs_8_), channel_id=1, source_target_pairs={{0,2},{2,0},{4,6},{6,4},{8,10},{10,8},{12,14},{14,12},{1,3},{3,1},... | collective-permute-start | bytes 368648 | tf_op jit(solution)/shard_map/ppermute | solution.py:158
  92.2 0.6 collective-permute-done.27.refs_14_
  92.8 1.2 %collective-permute-start.24 = (bf16[96,640]{1,0:T(8,128)(2,1)S(1)}, bf16[96,640]{1,0:T(8,128)(2,1)S(1)}, u32[]{:S(2)}, u32[]{:S(2)}) collective-permute-start(bf16[96,640]{1,0:T(8,128)(2,1)S(1)} %collective-permute-done.23.refs_10_), channel_id=1, source_target_pairs={{0,2},{2,0},{4,6},{6,4},{8,10},{10,8},{12,14},{14,12},{1,3},{3,1},... | collective-permute-start | bytes 368648 | tf_op jit(solution)/shard_map/ppermute | solution.py:158
  95.5 1.5 %shard_map.109 = bf16[24,4,5120]{2,1,0:T(4,128)(2,1)} custom-call(bf16[48,640]{1,0:T(8,128)(2,1)S(1)} %get-tuple-element.46.refs_0_, bf16[48,640]{1,0:T(8,128)(2,1)S(1)} %collective-permute-done.14.refs_1_, bf16[96,640]{1,0:T(8,128)(2,1)S(1)} %collective-permute-done.15.refs_2_, bf16[96,640]{1,0:T(8,128)(2,1)S(1)} %collective-permute-done.16.refs_3_, ...), custom_call_target="tpu_custom_call" | custom-call | tf_op jit(solution)/shard_map/pallas_call | solution.py:419
  (62 shorter events, 3.3 us)
Async XLA Ops:
  0.0 15.9 %copy-start = (f32[1,8,320]{2,1,0:T(8,128)S(1)}, f32[1,8,320]{2,1,0:T(8,128)}, u32[]{:S(2)}) copy-start(f32[1,8,320]{2,1,0:T(8,128)} %param.14) | copy-start | bytes 30724
  0.0 5.2 %copy-start.1 = (bf16[192,1,8,320]{3,2,1,0:T(8,128)(2,1)S(1)}, bf16[192,1,8,320]{3,2,1,0:T(8,128)(2,1)}, u32[]{:S(2)}) copy-start(bf16[192,1,8,320]{3,2,1,0:T(8,128)(2,1)} %param.10) | copy-start | bytes 2949124
  2.8 18.3 %collective-permute-start.4 = (bf16[192,640]{1,0:T(8,128)(2,1)}, bf16[192,640]{1,0:T(8,128)(2,1)S(1)}, u32[]{:S(2)}, u32[]{:S(2)}) collective-permute-start(bf16[192,640]{1,0:T(8,128)(2,1)} %get-tuple-element.37), channel_id=1, source_target_pairs={{0,12},{2,14},{4,8},{6,10},{8,4},{10,6},{12,0},{14,2},{1,13},{3,15... | collective-permute-start | bytes 737288 | tf_op jit(solution)/shard_map/ppermute | solution.py:158
  4.1 20.7 %collective-permute-start.3 = (bf16[192,640]{1,0:T(8,128)(2,1)S(1)}, bf16[192,640]{1,0:T(8,128)(2,1)S(1)}, u32[]{:S(2)}, u32[]{:S(2)}) collective-permute-start(bf16[192,640]{1,0:T(8,128)(2,1)S(1)} %get-tuple-element.30.rest_1_), channel_id=1, source_target_pairs={{0,8},{2,10},{4,12},{6,14},{8,0},{10,2},{12,4},{14,6},{1,9},{3,11}... | collective-permute-start | bytes 737288 | tf_op jit(solution)/shard_map/ppermute | solution.py:158
  5.2 1.3 %copy-start.3 = (bf16[192,1,8,320]{3,2,1,0:T(8,128)(2,1)S(1)}, bf16[192,1,8,320]{3,2,1,0:T(8,128)(2,1)}, u32[]{:S(2)}) copy-start(bf16[192,1,8,320]{3,2,1,0:T(8,128)(2,1)} %param.11) | copy-start | bytes 2949124
  6.5 0.7 copy-start.9
  8.9 0.7 copy-start.7
  9.6 8.1 %collective-permute-start = (bf16[192,640]{1,0:T(8,128)(2,1)}, bf16[192,640]{1,0:T(8,128)(2,1)S(1)}, u32[]{:S(2)}, u32[]{:S(2)}) collective-permute-start(bf16[192,640]{1,0:T(8,128)(2,1)} %get-tuple-element.32), channel_id=1, source_target_pairs={{0,2},{2,0},{4,6},{6,4},{8,10},{10,8},{12,14},{14,12},{1,3},{3,1},... | collective-permute-start | bytes 737288 | tf_op jit(solution)/shard_map/ppermute | solution.py:158
  10.7 14.2 %collective-permute-start.1 = (bf16[192,640]{1,0:T(8,128)(2,1)}, bf16[192,640]{1,0:T(8,128)(2,1)S(1)}, u32[]{:S(2)}, u32[]{:S(2)}) collective-permute-start(bf16[192,640]{1,0:T(8,128)(2,1)} %get-tuple-element.35), channel_id=1, source_target_pairs={{0,4},{2,6},{4,0},{6,2},{8,12},{10,14},{12,8},{14,10},{1,5},{3,7},... | collective-permute-start | bytes 737288 | tf_op jit(solution)/shard_map/ppermute | solution.py:158
  11.6 17.0 %collective-permute-start.2 = (bf16[192,640]{1,0:T(8,128)(2,1)}, bf16[192,640]{1,0:T(8,128)(2,1)S(1)}, u32[]{:S(2)}, u32[]{:S(2)}) collective-permute-start(bf16[192,640]{1,0:T(8,128)(2,1)} %get-tuple-element.36), channel_id=1, source_target_pairs={{0,6},{2,4},{4,2},{6,0},{8,14},{10,12},{12,10},{14,8},{1,7},{3,5},... | collective-permute-start | bytes 737288 | tf_op jit(solution)/shard_map/ppermute | solution.py:158
  13.4 1.2 %copy-start.6 = (bf16[24,4,1,5120]{3,1,2,0:T(4,128)(2,1)S(1)}, bf16[24,4,1,5120]{3,1,2,0:T(4,128)(2,1)}, u32[]{:S(2)}) copy-start(bf16[24,4,1,5120]{3,1,2,0:T(4,128)(2,1)} %param.16) | copy-start | bytes 2949124
  14.6 0.7 copy-start.11
  16.0 1.7 %copy-start.8 = (bf16[192,640]{1,0:T(8,128)(2,1)S(1)}, bf16[192,640]{1,0:T(8,128)(2,1)}, u32[]{:S(2)}) copy-start(bf16[192,640]{1,0:T(8,128)(2,1)} %copy-done.7) | copy-start | bytes 737284
  16.0 2.9 %copy-start.5 = (bf16[192,1,8,320]{3,2,1,0:T(8,128)(2,1)S(1)}, bf16[192,1,8,320]{3,2,1,0:T(8,128)(2,1)}, u32[]{:S(2)}) copy-start(bf16[192,1,8,320]{3,2,1,0:T(8,128)(2,1)} %param.9) | copy-start | bytes 2949124
  17.6 1.3 %copy-start.2 = (bf16[192,1,8,320]{3,2,1,0:T(8,128)(2,1)S(1)}, bf16[192,1,8,320]{3,2,1,0:T(8,128)(2,1)}, u32[]{:S(2)}) copy-start(bf16[192,1,8,320]{3,2,1,0:T(8,128)(2,1)} %param.10) | copy-start | bytes 2949124
  17.6 1.7 %copy-start.4 = (bf16[192,1,8,320]{3,2,1,0:T(8,128)(2,1)S(1)}, bf16[192,1,8,320]{3,2,1,0:T(8,128)(2,1)}, u32[]{:S(2)}) copy-start(bf16[192,1,8,320]{3,2,1,0:T(8,128)(2,1)} %param.11) | copy-start | bytes 2949124
  17.6 1.7 %copy-start.10 = (f32[1,8,192]{2,1,0:T(8,128)S(1)}, f32[1,8,192]{2,1,0:T(8,128)}, u32[]{:S(2)}) copy-start(f32[1,8,192]{2,1,0:T(8,128)} %param.12) | copy-start | bytes 18436
  29.9 30.9 %collective-permute-start.13 = (bf16[480,640]{1,0:T(8,128)(2,1)S(1)}, bf16[480,640]{1,0:T(8,128)(2,1)S(1)}, u32[]{:S(2)}, u32[]{:S(2)}) collective-permute-start(bf16[480,640]{1,0:T(8,128)(2,1)S(1)} %shard_map.101.refs_3_), channel_id=1, source_target_pairs={{0,8},{2,10},{4,12},{6,14},{8,0},{10,2},{12,4},{14,6},{1,9},{3,11}... | collective-permute-start | bytes 1843208 | tf_op jit(solution)/shard_map/ppermute | solution.py:158
  33.1 2.0 %collective-permute-start.9 = (bf16[192,640]{1,0:T(8,128)(2,1)S(1)}, bf16[192,640]{1,0:T(8,128)(2,1)S(1)}, u32[]{:S(2)}, u32[]{:S(2)}) collective-permute-start(bf16[192,640]{1,0:T(8,128)(2,1)S(1)} %shard_map.100.refs_6_), channel_id=1, source_target_pairs={{0,2},{2,0},{4,6},{6,4},{8,10},{10,8},{12,14},{14,12},{1,3},{3,1},... | collective-permute-start | bytes 737288 | tf_op jit(solution)/shard_map/ppermute | solution.py:158
  33.8 19.0 %collective-permute-start.6 = (bf16[192,640]{1,0:T(8,128)(2,1)S(1)}, bf16[192,640]{1,0:T(8,128)(2,1)S(1)}, u32[]{:S(2)}, u32[]{:S(2)}) collective-permute-start(bf16[192,640]{1,0:T(8,128)(2,1)S(1)} %shard_map.97.refs_8_), channel_id=1, source_target_pairs={{0,6},{2,4},{4,2},{6,0},{8,14},{10,12},{12,10},{14,8},{1,7},{3,5},... | collective-permute-start | bytes 737288 | tf_op jit(solution)/shard_map/ppermute | solution.py:158
  33.8 22.7 %collective-permute-start.5 = (bf16[192,640]{1,0:T(8,128)(2,1)S(1)}, bf16[192,640]{1,0:T(8,128)(2,1)S(1)}, u32[]{:S(2)}, u32[]{:S(2)}) collective-permute-start(bf16[192,640]{1,0:T(8,128)(2,1)S(1)} %shard_map.96.refs_7_), channel_id=1, source_target_pairs={{0,4},{2,6},{4,0},{6,2},{8,12},{10,14},{12,8},{14,10},{1,5},{3,7},... | collective-permute-start | bytes 737288 | tf_op jit(solution)/shard_map/ppermute | solution.py:158
  36.4 24.4 %collective-permute-start.11 = (bf16[192,640]{1,0:T(8,128)(2,1)S(1)}, bf16[192,640]{1,0:T(8,128)(2,1)S(1)}, u32[]{:S(2)}, u32[]{:S(2)}) collective-permute-start(bf16[192,640]{1,0:T(8,128)(2,1)S(1)} %shard_map.104.refs_2_), channel_id=1, source_target_pairs={{0,2},{2,0},{4,6},{6,4},{8,10},{10,8},{12,14},{14,12},{1,3},{3,1},... | collective-permute-start | bytes 737288 | tf_op jit(solution)/shard_map/ppermute | solution.py:158
  37.2 23.5 %collective-permute-start.12 = (bf16[192,640]{1,0:T(8,128)(2,1)S(1)}, bf16[192,640]{1,0:T(8,128)(2,1)S(1)}, u32[]{:S(2)}, u32[]{:S(2)}) collective-permute-start(bf16[192,640]{1,0:T(8,128)(2,1)S(1)} %shard_map.105.refs_4_), channel_id=1, source_target_pairs={{0,2},{2,0},{4,6},{6,4},{8,10},{10,8},{12,14},{14,12},{1,3},{3,1},... | collective-permute-start | bytes 737288 | tf_op jit(solution)/shard_map/ppermute | solution.py:158
  52.8 3.7 %collective-permute-start.10 = (bf16[96,640]{1,0:T(8,128)(2,1)S(1)}, bf16[96,640]{1,0:T(8,128)(2,1)S(1)}, u32[]{:S(2)}, u32[]{:S(2)}) collective-permute-start(bf16[96,640]{1,0:T(8,128)(2,1)S(1)} %shard_map.103), channel_id=1, source_target_pairs={{0,2},{2,0},{4,6},{6,4},{8,10},{10,8},{12,14},{14,12},{1,3},{3,1},... | collective-permute-start | bytes 368648 | tf_op jit(solution)/shard_map/ppermute | solution.py:158
  56.5 9.2 %collective-permute-start.7 = (bf16[96,640]{1,0:T(8,128)(2,1)S(1)}, bf16[96,640]{1,0:T(8,128)(2,1)S(1)}, u32[]{:S(2)}, u32[]{:S(2)}) collective-permute-start(bf16[96,640]{1,0:T(8,128)(2,1)S(1)} %shard_map.98), channel_id=1, source_target_pairs={{0,4},{2,6},{4,0},{6,2},{8,12},{10,14},{12,8},{14,10},{1,5},{3,7},... | collective-permute-start | bytes 368648 | tf_op jit(solution)/shard_map/ppermute | solution.py:158
  56.5 9.2 %collective-permute-start.8 = (bf16[96,640]{1,0:T(8,128)(2,1)S(1)}, bf16[96,640]{1,0:T(8,128)(2,1)S(1)}, u32[]{:S(2)}, u32[]{:S(2)}) collective-permute-start(bf16[96,640]{1,0:T(8,128)(2,1)S(1)} %shard_map.99), channel_id=1, source_target_pairs={{0,6},{2,4},{4,2},{6,0},{8,14},{10,12},{12,10},{14,8},{1,7},{3,5},... | collective-permute-start | bytes 368648 | tf_op jit(solution)/shard_map/ppermute | solution.py:158
  68.1 7.4 %collective-permute-start.15 = (bf16[96,640]{1,0:T(8,128)(2,1)S(1)}, bf16[96,640]{1,0:T(8,128)(2,1)S(1)}, u32[]{:S(2)}, u32[]{:S(2)}) collective-permute-start(bf16[96,640]{1,0:T(8,128)(2,1)S(1)} %get-tuple-element.48), channel_id=1, source_target_pairs={{0,8},{1,9},{2,10},{3,11},{4,12},{5,13},{6,14},{7,15},{8,0},{9,1},... | collective-permute-start | bytes 368648 | tf_op jit(solution)/shard_map/ppermute | solution.py:149
  69.7 6.9 %collective-permute-start.17 = (bf16[96,640]{1,0:T(8,128)(2,1)S(1)}, bf16[96,640]{1,0:T(8,128)(2,1)S(1)}, u32[]{:S(2)}, u32[]{:S(2)}) collective-permute-start(bf16[96,640]{1,0:T(8,128)(2,1)S(1)} %get-tuple-element.49), channel_id=1, source_target_pairs={{0,1},{1,0},{2,3},{3,2},{4,5},{5,4},{6,7},{7,6},{8,9},{9,8},{10,11... | collective-permute-start | bytes 368648 | tf_op jit(solution)/shard_map/ppermute | solution.py:149
  70.9 6.8 %collective-permute-start.19 = (bf16[96,640]{1,0:T(8,128)(2,1)S(1)}, bf16[96,640]{1,0:T(8,128)(2,1)S(1)}, u32[]{:S(2)}, u32[]{:S(2)}) collective-permute-start(bf16[96,640]{1,0:T(8,128)(2,1)S(1)} %get-tuple-element.50), channel_id=1, source_target_pairs={{0,4},{1,5},{2,6},{3,7},{4,0},{5,1},{6,2},{7,3},{8,12},{9,13},{10,... | collective-permute-start | bytes 368648 | tf_op jit(solution)/shard_map/ppermute | solution.py:149
  71.5 9.4 %collective-permute-start.21 = (bf16[96,640]{1,0:T(8,128)(2,1)S(1)}, bf16[96,640]{1,0:T(8,128)(2,1)S(1)}, u32[]{:S(2)}, u32[]{:S(2)}) collective-permute-start(bf16[96,640]{1,0:T(8,128)(2,1)S(1)} %get-tuple-element.51), channel_id=1, source_target_pairs={{0,5},{1,4},{2,7},{3,6},{4,1},{5,0},{6,3},{7,2},{8,13},{9,12},{10,... | collective-permute-start | bytes 368648 | tf_op jit(solution)/shard_map/ppermute | solution.py:149
  72.3 2.4 %collective-permute-start.14 = (bf16[48,640]{1,0:T(8,128)(2,1)S(1)}, bf16[48,640]{1,0:T(8,128)(2,1)S(1)}, u32[]{:S(2)}, u32[]{:S(2)}) collective-permute-start(bf16[48,640]{1,0:T(8,128)(2,1)S(1)} %get-tuple-element.47), channel_id=1, source_target_pairs={{0,2},{2,0},{4,6},{6,4},{8,10},{10,8},{12,14},{14,12},{1,3},{3,1},... | collective-permute-start | bytes 184328 | tf_op jit(solution)/shard_map/ppermute | solution.py:158
  74.7 8.3 %collective-permute-start.23 = (bf16[96,640]{1,0:T(8,128)(2,1)S(1)}, bf16[96,640]{1,0:T(8,128)(2,1)S(1)}, u32[]{:S(2)}, u32[]{:S(2)}) collective-permute-start(bf16[96,640]{1,0:T(8,128)(2,1)S(1)} %get-tuple-element.52), channel_id=1, source_target_pairs={{0,9},{1,8},{2,11},{3,10},{4,13},{5,12},{6,15},{7,14},{8,1},{9,0},... | collective-permute-start | bytes 368648 | tf_op jit(solution)/shard_map/ppermute | solution.py:149
  75.5 14.8 %collective-permute-start.25 = (bf16[96,640]{1,0:T(8,128)(2,1)S(1)}, bf16[96,640]{1,0:T(8,128)(2,1)S(1)}, u32[]{:S(2)}, u32[]{:S(2)}) collective-permute-start(bf16[96,640]{1,0:T(8,128)(2,1)S(1)} %get-tuple-element.53), channel_id=1, source_target_pairs={{0,12},{1,13},{2,14},{3,15},{4,8},{5,9},{6,10},{7,11},{8,4},{9,5},... | collective-permute-start | bytes 368648 | tf_op jit(solution)/shard_map/ppermute | solution.py:149
  76.6 16.2 %collective-permute-start.27 = (bf16[96,640]{1,0:T(8,128)(2,1)S(1)}, bf16[96,640]{1,0:T(8,128)(2,1)S(1)}, u32[]{:S(2)}, u32[]{:S(2)}) collective-permute-start(bf16[96,640]{1,0:T(8,128)(2,1)S(1)} %get-tuple-element.54), channel_id=1, source_target_pairs={{0,13},{1,12},{2,15},{3,14},{4,9},{5,8},{6,11},{7,10},{8,5},{9,4},... | collective-permute-start | bytes 368648 | tf_op jit(solution)/shard_map/ppermute | solution.py:149
  77.7 16.3 %collective-permute-start.16 = (bf16[96,640]{1,0:T(8,128)(2,1)S(1)}, bf16[96,640]{1,0:T(8,128)(2,1)S(1)}, u32[]{:S(2)}, u32[]{:S(2)}) collective-permute-start(bf16[96,640]{1,0:T(8,128)(2,1)S(1)} %collective-permute-done.15.refs_2_), channel_id=1, source_target_pairs={{0,2},{2,0},{4,6},{6,4},{8,10},{10,8},{12,14},{14,12},{1,3},{3,1},... | collective-permute-start | bytes 368648 | tf_op jit(solution)/shard_map/ppermute | solution.py:158
  80.8 13.2 %collective-permute-start.18 = (bf16[96,640]{1,0:T(8,128)(2,1)S(1)}, bf16[96,640]{1,0:T(8,128)(2,1)S(1)}, u32[]{:S(2)}, u32[]{:S(2)}) collective-permute-start(bf16[96,640]{1,0:T(8,128)(2,1)S(1)} %collective-permute-done.17.refs_4_), channel_id=1, source_target_pairs={{0,2},{2,0},{4,6},{6,4},{8,10},{10,8},{12,14},{14,12},{1,3},{3,1},... | collective-permute-start | bytes 368648 | tf_op jit(solution)/shard_map/ppermute | solution.py:158
  83.0 11.5 %collective-permute-start.20 = (bf16[96,640]{1,0:T(8,128)(2,1)S(1)}, bf16[96,640]{1,0:T(8,128)(2,1)S(1)}, u32[]{:S(2)}, u32[]{:S(2)}) collective-permute-start(bf16[96,640]{1,0:T(8,128)(2,1)S(1)} %collective-permute-done.19.refs_6_), channel_id=1, source_target_pairs={{0,2},{2,0},{4,6},{6,4},{8,10},{10,8},{12,14},{14,12},{1,3},{3,1},... | collective-permute-start | bytes 368648 | tf_op jit(solution)/shard_map/ppermute | solution.py:158
  90.3 4.2 %collective-permute-start.22 = (bf16[96,640]{1,0:T(8,128)(2,1)S(1)}, bf16[96,640]{1,0:T(8,128)(2,1)S(1)}, u32[]{:S(2)}, u32[]{:S(2)}) collective-permute-start(bf16[96,640]{1,0:T(8,128)(2,1)S(1)} %collective-permute-done.21.refs_8_), channel_id=1, source_target_pairs={{0,2},{2,0},{4,6},{6,4},{8,10},{10,8},{12,14},{14,12},{1,3},{3,1},... | collective-permute-start | bytes 368648 | tf_op jit(solution)/shard_map/ppermute | solution.py:158
  92.8 2.2 %collective-permute-start.24 = (bf16[96,640]{1,0:T(8,128)(2,1)S(1)}, bf16[96,640]{1,0:T(8,128)(2,1)S(1)}, u32[]{:S(2)}, u32[]{:S(2)}) collective-permute-start(bf16[96,640]{1,0:T(8,128)(2,1)S(1)} %collective-permute-done.23.refs_10_), channel_id=1, source_target_pairs={{0,2},{2,0},{4,6},{6,4},{8,10},{10,8},{12,14},{14,12},{1,3},{3,1},... | collective-permute-start | bytes 368648 | tf_op jit(solution)/shard_map/ppermute | solution.py:158
  94.0 1.3 %collective-permute-start.26 = (bf16[96,640]{1,0:T(8,128)(2,1)S(1)}, bf16[96,640]{1,0:T(8,128)(2,1)S(1)}, u32[]{:S(2)}, u32[]{:S(2)}) collective-permute-start(bf16[96,640]{1,0:T(8,128)(2,1)S(1)} %collective-permute-done.25.refs_12_), channel_id=1, source_target_pairs={{0,2},{2,0},{4,6},{6,4},{8,10},{10,8},{12,14},{14,12},{1,3},{3,1},... | collective-permute-start | bytes 368648 | tf_op jit(solution)/shard_map/ppermute | solution.py:158
  94.0 1.5 %collective-permute-start.28 = (bf16[96,640]{1,0:T(8,128)(2,1)S(1)}, bf16[96,640]{1,0:T(8,128)(2,1)S(1)}, u32[]{:S(2)}, u32[]{:S(2)}) collective-permute-start(bf16[96,640]{1,0:T(8,128)(2,1)S(1)} %collective-permute-done.27.refs_14_), channel_id=1, source_target_pairs={{0,2},{2,0},{4,6},{6,4},{8,10},{10,8},{12,14},{14,12},{1,3},{3,1},... | collective-permute-start | bytes 368648 | tf_op jit(solution)/shard_map/ppermute | solution.py:158

commit v2 on v1

--- a/solution.py
+++ b/solution.py
@@ -362,8 +362,11 @@
                 )
 
 
-def silu_kernel(gate_ref, out_ref):
+def silu_kernel(gate_any, out_ref, gate_ref, sem):
     height, frames_here, channels = gate_ref.shape
+    copy = pltpu.make_async_copy(gate_any, gate_ref, sem)
+    copy.start()
+    copy.wait()
     gate = gate_ref[...].astype(jnp.float32)
     out_ref[...] = (gate * jax.nn.sigmoid(gate)).reshape(height * frames_here, channels)
 
@@ -506,7 +509,9 @@
     opened = call(
         silu_kernel,
         jax.ShapeDtypeStruct((height * frames_here, gate_input.shape[3]), jnp.float32),
-        (gate,),
+        (pltpu.with_memory_space_constraint(gate, pltpu.HBM),),
+        (pltpu.VMEM(gate.shape, jnp.bfloat16), pltpu.SemaphoreType.DMA(())),
+        specs=[pl.BlockSpec(memory_space=pltpu.HBM)],
     )
     early = (opened, across[0], own_weights, own_gain, own_taps, frames, mirror_sum)
     query_struct = jax.ShapeDtypeStruct((half, wide), jnp.bfloat16)

time: 97.6 us -> 97.5 us (level)
  local copies, waits for them, and re-layouts: 7.93 us -> 6.43 us
  Pallas kernels: 20.3 us -> 21.5 us
    unnamed x25 -> x23, local copies, waits for them, and re-layouts: 4.57 us -> 3.07 us
    pallas_call x11, Pallas kernels: 20.3 us -> 21.5 us  [call(): pl.pallas_call(kernel, out_shape=out, in_specs=specs, out_specs=jax.tree....]
  transfers between devices with their start and end apart: 29 -> 29, of which waited for: 12 -> 12; matrix products, arithmetic and copies ran while one was open for 3% -> 3% of each run, Pallas kernels for 13% -> 14%
where the time goes in v2:
time: 97.5 us; the launch traced here: 97.2 us
  starting transfers between devices  34.7 us (36%)
  waiting for transfers between devices  34.1 us (35%)
  Pallas kernels  21.5 us (22%)
  local copies, waits for them, and re-layouts  6.43 us (7%)
    ppermute x22, waiting for transfers between devices, send(): return lax.ppermute(part, 'tok', pairs)  28.9 us
    ppermute x22, starting transfers between devices, send(): return lax.ppermute(part, 'tok', pairs)  27.5 us
    pallas_call x11, Pallas kernels, call(): pl.pallas_call(kernel, out_shape=out, in_specs=specs, out_specs=jax.tree....  21.5 us
    ppermute x7, starting transfers between devices, send_far(): return lax.ppermute(part, ('tok', 'head'), pairs)  7.23 us
    ppermute x7, waiting for transfers between devices, send_far(): return lax.ppermute(part, ('tok', 'head'), pairs)  5.17 us
    unnamed x23, local copies, waits for them, and re-layouts  3.07 us
  transfers between devices with their start and end apart: 29, of which 12 were waited for; matrix products, arithmetic and copies ran while one was open for 3% of the time, Pallas kernels for 14%

profile of v2, /device:TPU:13, one launch (start us, length us, event | category | flops | bytes accessed | tf_op | source)
XLA Modules:
  0.0 97.2 jit_solution(7136718145573752773)
XLA Ops:
  0.0 2.8 %shard_map.92 = (bf16[192,640]{1,0:T(8,128)(2,1)S(1)}, bf16[192,640]{1,0:T(8,128)(2,1)}) custom-call(bf16[192,8,320]{2,1,0:T(8,128)(2,1)} %bitcast.23), custom_call_target="tpu_custom_call" | custom-call | tf_op jit(solution)/shard_map/pallas_call | solution.py:422
  2.8 1.4 %collective-permute-start.4 = (bf16[192,640]{1,0:T(8,128)(2,1)}, bf16[192,640]{1,0:T(8,128)(2,1)S(1)}, u32[]{:S(2)}, u32[]{:S(2)}) collective-permute-start(bf16[192,640]{1,0:T(8,128)(2,1)} %get-tuple-element.37), channel_id=1, source_target_pairs={{0,12},{2,14},{4,8},{6,10},{8,4},{10,6},{12,0},{14,2},{1,13},{3,15... | collective-permute-start | bytes 737288 | tf_op jit(solution)/shard_map/ppermute | solution.py:158
  4.1 1.1 %collective-permute-start.3 = (bf16[192,640]{1,0:T(8,128)(2,1)S(1)}, bf16[192,640]{1,0:T(8,128)(2,1)S(1)}, u32[]{:S(2)}, u32[]{:S(2)}) collective-permute-start(bf16[192,640]{1,0:T(8,128)(2,1)S(1)} %get-tuple-element.30.rest_1_), channel_id=1, source_target_pairs={{0,8},{2,10},{4,12},{6,14},{8,0},{10,2},{12,4},{14,6},{1,9},{3,11}... | collective-permute-start | bytes 737288 | tf_op jit(solution)/shard_map/ppermute | solution.py:158
  5.2 1.3 %copy-done.3 = bf16[192,1,8,320]{3,2,1,0:T(8,128)(2,1)S(1)} copy-done((bf16[192,1,8,320]{3,2,1,0:T(8,128)(2,1)S(1)}, bf16[192,1,8,320]{3,2,1,0:T(8,128)(2,1)}, u32[]{:S(2)}) %copy-start.3) | copy-done | bytes 983064
  6.5 0.7 copy-done.8
  7.2 1.7 %shard_map.93 = (bf16[192,640]{1,0:T(8,128)(2,1)S(1)}, bf16[192,640]{1,0:T(8,128)(2,1)}, bf16[192,640]{1,0:T(8,128)(2,1)}, bf16[192,640]{1,0:T(8,128)(2,1)}) custom-call(bf16[192,8,320]{2,1,0:T(8,128)(2,1)S(1)} %bitcast.19, bf16[192,8,320]{2,1,0:T(8,128)(2,1)S(1)} %bitcast.21, f32[8,192]{1,0:T(8,128)S(1)} %bitcast.25), custom_call_target="tpu_custom_call" | custom-call | tf_op jit(solution)/shard_map/pallas_call | solution.py:422
  8.9 0.7 copy-done.6
  9.6 1.1 %collective-permute-start = (bf16[192,640]{1,0:T(8,128)(2,1)}, bf16[192,640]{1,0:T(8,128)(2,1)S(1)}, u32[]{:S(2)}, u32[]{:S(2)}) collective-permute-start(bf16[192,640]{1,0:T(8,128)(2,1)} %get-tuple-element.32), channel_id=1, source_target_pairs={{0,2},{2,0},{4,6},{6,4},{8,10},{10,8},{12,14},{14,12},{1,3},{3,1},... | collective-permute-start | bytes 737288 | tf_op jit(solution)/shard_map/ppermute | solution.py:158
  10.7 1.0 collective-permute-start.1
  11.6 0.7 collective-permute-start.2
  12.3 1.1 %reshape.53 = f32[9,16,320]{2,1,0:T(8,128)S(1)} reshape(f32[3,3,5120]{2,1,0:T(4,128)} %param.17) | data formatting | bytes 368640 | tf_op jit(solution)/shard_map/reshape | solution.py:496
  13.4 1.6 %shard_map.91.rest_0_.refs_16_ = f32[96,5120]{1,0:T(8,128)S(1)} custom-call(bf16[24,4,5120]{2,1,0:T(4,128)(2,1)} %bitcast.27), custom_call_target="tpu_custom_call" | custom-call | tf_op jit(solution)/shard_map/pallas_call | solution.py:422
  15.0 0.6 gather_fusion
  15.7 1.6 %dynamic-slice_bitcast_fusion = (bf16[3,320,320]{2,1,0:T(8,128)(2,1)S(1)}, bf16[3,320,320]{2,1,0:T(8,128)(2,1)S(1)}) fusion(bf16[1,8,3,320,320]{4,3,2,1,0:T(8,128)(2,1)} %param.13, s32[]{:T(128)S(6)} %select_n.26, s32[]{:T(128)S(6)} %select_n.24), kind=kLoop, calls=%fused_computation.1 | loop fusion | bytes 2457608 | tf_op jit(solution)/shard_map/jit(dynamic_index_in_dim)/squeeze | solution.py:465
  17.4 1.2 %shard_map.94.rest_6_.refs_3_ = f32[3,320,384]{2,1,0:T(8,128)S(1)} custom-call(bf16[192,640]{1,0:T(8,128)(2,1)S(1)} %copy-done.7, bf16[192,640]{1,0:T(8,128)(2,1)S(1)} %collective-permute-done.refs_1_, bf16[3,320,320]{2,1,0:T(8,128)(2,1)S(1)} %get-tuple-element.55.refs_2_), custom_call_target="tpu_custom_call" | custom-call | tf_op jit(solution)/shard_map/pallas_call | solution.py:422
  19.0 1.8 %shard_map.95 = (bf16[192,640]{1,0:T(8,128)(2,1)S(1)}, bf16[192,640]{1,0:T(8,128)(2,1)S(1)}, bf16[192,640]{1,0:T(8,128)(2,1)S(1)}, bf16[192,640]{1,0:T(8,128)(2,...) custom-call(bf16[192,8,320]{2,1,0:T(8,128)(2,1)S(1)} %bitcast.20, ...), custom_call_target="tpu_custom_call" | custom-call | tf_op jit(solution)/shard_map/pallas_call | solution.py:422
  20.8 4.0 %collective-permute-done.3.refs_4_.refs_0_ = bf16[192,640]{1,0:T(8,128)(2,1)S(1)} collective-permute-done((bf16[192,640]{1,0:T(8,128)(2,1)S(1)}, bf16[192,640]{1,0:T(8,128)(2,1)S(1)}, u32[]{:S(2)}, u32[]{:S(2)}) %collective-permute-start.3) | collective-permute-done | bytes 245792 | tf_op jit(solution)/shard_map/ppermute | solution.py:158
  24.8 3.8 %collective-permute-done.2.refs_3_.refs_1_ = bf16[192,640]{1,0:T(8,128)(2,1)S(1)} collective-permute-done((bf16[192,640]{1,0:T(8,128)(2,1)}, bf16[192,640]{1,0:T(8,128)(2,1)S(1)}, u32[]{:S(2)}, u32[]{:S(2)}) %collective-permute-start.2) | collective-permute-done | bytes 245792 | tf_op jit(solution)/shard_map/ppermute | solution.py:158
  28.6 1.3 %shard_map.101.refs_3_ = bf16[480,640]{1,0:T(8,128)(2,1)S(1)} custom-call(bf16[192,640]{1,0:T(8,128)(2,1)S(1)} %collective-permute-done.1.refs_2_.refs_0_, bf16[192,640]{1,0:T(8,128)(2,1)S(1)} %collective-permute-done.2.refs_3_.refs_1_, bf16[3,320,320]{2,1,0:T(8,128)(2,1)S(1)} %get-tuple-element.55.refs_2_, f32[3,320,384]{2,1,0:T(8,128)S(1)} %shard_map.94.rest_6_.refs_3_, ...), custom_call_target="tpu_custom_call" | custom-call | tf_op jit(solution)/shard_map/pallas_call | solution.py:422
  29.9 3.2 %collective-permute-start.13 = (bf16[480,640]{1,0:T(8,128)(2,1)S(1)}, bf16[480,640]{1,0:T(8,128)(2,1)S(1)}, u32[]{:S(2)}, u32[]{:S(2)}) collective-permute-start(bf16[480,640]{1,0:T(8,128)(2,1)S(1)} %shard_map.101.refs_3_), channel_id=1, source_target_pairs={{0,8},{2,10},{4,12},{6,14},{8,0},{10,2},{12,4},{14,6},{1,9},{3,11}... | collective-permute-start | bytes 1843208 | tf_op jit(solution)/shard_map/ppermute | solution.py:158
  33.1 0.7 collective-permute-start.9
  33.8 1.4 %collective-permute-start.5 = (bf16[192,640]{1,0:T(8,128)(2,1)S(1)}, bf16[192,640]{1,0:T(8,128)(2,1)S(1)}, u32[]{:S(2)}, u32[]{:S(2)}) collective-permute-start(bf16[192,640]{1,0:T(8,128)(2,1)S(1)} %shard_map.96.refs_7_), channel_id=1, source_target_pairs={{0,4},{2,6},{4,0},{6,2},{8,12},{10,14},{12,8},{14,10},{1,5},{3,7},... | collective-permute-start | bytes 737288 | tf_op jit(solution)/shard_map/ppermute | solution.py:158
  35.1 1.2 %shard_map.102.refs_1_.refs_3_ = f32[3,320,384]{2,1,0:T(8,128)S(1)} custom-call(bf16[192,640]{1,0:T(8,128)(2,1)S(1)} %get-tuple-element.42.refs_0_, bf16[192,640]{1,0:T(8,128)(2,1)S(1)} %collective-permute-done.9.refs_1_, bf16[3,320,320]{2,1,0:T(8,128)(2,1)S(1)} %get-tuple-element.56.rest_2_.refs_2_.refs_6_, bf16[480,640]{1,0:T(8,128)(2,1)S(1)} %shard_map.101.refs_3_), custom_call_target="tpu_custom_call" | custom-call | tf_op jit(solution)/shard_map/pallas_call | solution.py:422
  36.4 0.9 collective-permute-start.11
  37.3 15.5 %collective-permute-done.6.refs_2_.refs_1_ = bf16[192,640]{1,0:T(8,128)(2,1)S(1)} collective-permute-done((bf16[192,640]{1,0:T(8,128)(2,1)S(1)}, bf16[192,640]{1,0:T(8,128)(2,1)S(1)}, u32[]{:S(2)}, u32[]{:S(2)}) %collective-permute-start.6) | collective-permute-done | bytes 245792 | tf_op jit(solution)/shard_map/ppermute | solution.py:158
  52.8 3.7 %collective-permute-done.5.refs_1_.refs_0_ = bf16[192,640]{1,0:T(8,128)(2,1)S(1)} collective-permute-done((bf16[192,640]{1,0:T(8,128)(2,1)S(1)}, bf16[192,640]{1,0:T(8,128)(2,1)S(1)}, u32[]{:S(2)}, u32[]{:S(2)}) %collective-permute-start.5) | collective-permute-done | bytes 245792 | tf_op jit(solution)/shard_map/ppermute | solution.py:158
  56.5 3.0 %collective-permute-start.8 = (bf16[96,640]{1,0:T(8,128)(2,1)S(1)}, bf16[96,640]{1,0:T(8,128)(2,1)S(1)}, u32[]{:S(2)}, u32[]{:S(2)}) collective-permute-start(bf16[96,640]{1,0:T(8,128)(2,1)S(1)} %shard_map.99), channel_id=1, source_target_pairs={{0,6},{2,4},{4,2},{6,0},{8,14},{10,12},{12,10},{14,8},{1,7},{3,5},... | collective-permute-start | bytes 368648 | tf_op jit(solution)/shard_map/ppermute | solution.py:158
  59.5 1.3 %shard_map.106.refs_7_ = f32[3,320,384]{2,1,0:T(8,128)S(1)} custom-call(bf16[192,640]{1,0:T(8,128)(2,1)S(1)} %collective-permute-done.5.refs_1_.refs_0_, bf16[192,640]{1,0:T(8,128)(2,1)S(1)} %collective-permute-done.6.refs_2_.refs_1_, bf16[3,320,320]{2,1,0:T(8,128)(2,1)S(1)} %get-tuple-element.56.rest_2_.refs_2_.refs_6_, ...), custom_call_target="tpu_custom_call" | custom-call | tf_op jit(solution)/shard_map/pallas_call | solution.py:422
  60.8 4.9 %shard_map.107 = (bf16[3,320,320]{2,1,0:T(8,128)(2,1)S(1)}, f32[2,8,3,96,128]{4,3,2,1,0:T(8,128)S(1)}) custom-call(s32[8]{0:T(128)S(1)} %gather_fusion, bf16[96,640]{1,0:T(8,128)(2,1)S(1)} %get-tuple-element.40.refs_0_, bf16[96,640]{1,0:T(8,128)(2,1)S(1)} %collective-permute-done.10.refs_1_, bf16[192,640]{1,0:T(8,128)(2,1)S(1)} %shard_map.104.refs_2_, ...), custom_call_target="tpu_custom_call" | custom-call | tf_op jit(solution)/shard_map/pallas_call | solution.py:422
  65.8 2.3 %shard_map.108 = (bf16[48,640]{1,0:T(8,128)(2,1)S(1)}, bf16[48,640]{1,0:T(8,128)(2,1)S(1)}, bf16[96,640]{1,0:T(8,128)(2,1)S(1)}, bf16[96,640]{1,0:T(8,128)(2,1)S...) custom-call(s32[8]{0:T(128)S(1)} %gather_fusion, ...), custom_call_target="tpu_custom_call" | custom-call | tf_op jit(solution)/shard_map/pallas_call | solution.py:422
  68.1 1.6 %collective-permute-start.15 = (bf16[96,640]{1,0:T(8,128)(2,1)S(1)}, bf16[96,640]{1,0:T(8,128)(2,1)S(1)}, u32[]{:S(2)}, u32[]{:S(2)}) collective-permute-start(bf16[96,640]{1,0:T(8,128)(2,1)S(1)} %get-tuple-element.48), channel_id=1, source_target_pairs={{0,8},{1,9},{2,10},{3,11},{4,12},{5,13},{6,14},{7,15},{8,0},{9,1},... | collective-permute-start | bytes 368648 | tf_op jit(solution)/shard_map/ppermute | solution.py:149
  69.7 1.2 %collective-permute-start.17 = (bf16[96,640]{1,0:T(8,128)(2,1)S(1)}, bf16[96,640]{1,0:T(8,128)(2,1)S(1)}, u32[]{:S(2)}, u32[]{:S(2)}) collective-permute-start(bf16[96,640]{1,0:T(8,128)(2,1)S(1)} %get-tuple-element.49), channel_id=1, source_target_pairs={{0,1},{1,0},{2,3},{3,2},{4,5},{5,4},{6,7},{7,6},{8,9},{9,8},{10,11... | collective-permute-start | bytes 368648 | tf_op jit(solution)/shard_map/ppermute | solution.py:149
  71.5 0.8 collective-permute-start.21
  72.3 1.5 %collective-permute-start.14 = (bf16[48,640]{1,0:T(8,128)(2,1)S(1)}, bf16[48,640]{1,0:T(8,128)(2,1)S(1)}, u32[]{:S(2)}, u32[]{:S(2)}) collective-permute-start(bf16[48,640]{1,0:T(8,128)(2,1)S(1)} %get-tuple-element.47), channel_id=1, source_target_pairs={{0,2},{2,0},{4,6},{6,4},{8,10},{10,8},{12,14},{14,12},{1,3},{3,1},... | collective-permute-start | bytes 184328 | tf_op jit(solution)/shard_map/ppermute | solution.py:158
  73.8 0.9 collective-permute-done.14.refs_1_
  74.7 0.8 collective-permute-start.23
  75.5 1.1 %collective-permute-start.25 = (bf16[96,640]{1,0:T(8,128)(2,1)S(1)}, bf16[96,640]{1,0:T(8,128)(2,1)S(1)}, u32[]{:S(2)}, u32[]{:S(2)}) collective-permute-start(bf16[96,640]{1,0:T(8,128)(2,1)S(1)} %get-tuple-element.53), channel_id=1, source_target_pairs={{0,12},{1,13},{2,14},{3,15},{4,8},{5,9},{6,10},{7,11},{8,4},{9,5},... | collective-permute-start | bytes 368648 | tf_op jit(solution)/shard_map/ppermute | solution.py:149
  76.6 1.1 %collective-permute-start.27 = (bf16[96,640]{1,0:T(8,128)(2,1)S(1)}, bf16[96,640]{1,0:T(8,128)(2,1)S(1)}, u32[]{:S(2)}, u32[]{:S(2)}) collective-permute-start(bf16[96,640]{1,0:T(8,128)(2,1)S(1)} %get-tuple-element.54), channel_id=1, source_target_pairs={{0,13},{1,12},{2,15},{3,14},{4,9},{5,8},{6,11},{7,10},{8,5},{9,4},... | collective-permute-start | bytes 368648 | tf_op jit(solution)/shard_map/ppermute | solution.py:149
  77.7 1.7 %collective-permute-start.16 = (bf16[96,640]{1,0:T(8,128)(2,1)S(1)}, bf16[96,640]{1,0:T(8,128)(2,1)S(1)}, u32[]{:S(2)}, u32[]{:S(2)}) collective-permute-start(bf16[96,640]{1,0:T(8,128)(2,1)S(1)} %collective-permute-done.15.refs_2_), channel_id=1, source_target_pairs={{0,2},{2,0},{4,6},{6,4},{8,10},{10,8},{12,14},{14,12},{1,3},{3,1},... | collective-permute-start | bytes 368648 | tf_op jit(solution)/shard_map/ppermute | solution.py:158
  79.4 1.4 %collective-permute-done.21.refs_8_ = bf16[96,640]{1,0:T(8,128)(2,1)S(1)} collective-permute-done((bf16[96,640]{1,0:T(8,128)(2,1)S(1)}, bf16[96,640]{1,0:T(8,128)(2,1)S(1)}, u32[]{:S(2)}, u32[]{:S(2)}) %collective-permute-start.21) | collective-permute-done | bytes 122912 | tf_op jit(solution)/shard_map/ppermute | solution.py:149
  80.8 1.5 %collective-permute-start.18 = (bf16[96,640]{1,0:T(8,128)(2,1)S(1)}, bf16[96,640]{1,0:T(8,128)(2,1)S(1)}, u32[]{:S(2)}, u32[]{:S(2)}) collective-permute-start(bf16[96,640]{1,0:T(8,128)(2,1)S(1)} %collective-permute-done.17.refs_4_), channel_id=1, source_target_pairs={{0,2},{2,0},{4,6},{6,4},{8,10},{10,8},{12,14},{14,12},{1,3},{3,1},... | collective-permute-start | bytes 368648 | tf_op jit(solution)/shard_map/ppermute | solution.py:158
  82.3 0.7 collective-permute-done.23.refs_10_
  83.0 4.8 %collective-permute-start.20 = (bf16[96,640]{1,0:T(8,128)(2,1)S(1)}, bf16[96,640]{1,0:T(8,128)(2,1)S(1)}, u32[]{:S(2)}, u32[]{:S(2)}) collective-permute-start(bf16[96,640]{1,0:T(8,128)(2,1)S(1)} %collective-permute-done.19.refs_6_), channel_id=1, source_target_pairs={{0,2},{2,0},{4,6},{6,4},{8,10},{10,8},{12,14},{14,12},{1,3},{3,1},... | collective-permute-start | bytes 368648 | tf_op jit(solution)/shard_map/ppermute | solution.py:158
  87.8 2.5 %collective-permute-done.25.refs_12_ = bf16[96,640]{1,0:T(8,128)(2,1)S(1)} collective-permute-done((bf16[96,640]{1,0:T(8,128)(2,1)S(1)}, bf16[96,640]{1,0:T(8,128)(2,1)S(1)}, u32[]{:S(2)}, u32[]{:S(2)}) %collective-permute-start.25) | collective-permute-done | bytes 122912 | tf_op jit(solution)/shard_map/ppermute | solution.py:149
  90.3 2.0 %collective-permute-start.22 = (bf16[96,640]{1,0:T(8,128)(2,1)S(1)}, bf16[96,640]{1,0:T(8,128)(2,1)S(1)}, u32[]{:S(2)}, u32[]{:S(2)}) collective-permute-start(bf16[96,640]{1,0:T(8,128)(2,1)S(1)} %collective-permute-done.21.refs_8_), channel_id=1, source_target_pairs={{0,2},{2,0},{4,6},{6,4},{8,10},{10,8},{12,14},{14,12},{1,3},{3,1},... | collective-permute-start | bytes 368648 | tf_op jit(solution)/shard_map/ppermute | solution.py:158
  92.2 0.6 collective-permute-done.27.refs_14_
  92.8 1.2 %collective-permute-start.24 = (bf16[96,640]{1,0:T(8,128)(2,1)S(1)}, bf16[96,640]{1,0:T(8,128)(2,1)S(1)}, u32[]{:S(2)}, u32[]{:S(2)}) collective-permute-start(bf16[96,640]{1,0:T(8,128)(2,1)S(1)} %collective-permute-done.23.refs_10_), channel_id=1, source_target_pairs={{0,2},{2,0},{4,6},{6,4},{8,10},{10,8},{12,14},{14,12},{1,3},{3,1},... | collective-permute-start | bytes 368648 | tf_op jit(solution)/shard_map/ppermute | solution.py:158
  95.5 1.5 %shard_map.109 = bf16[24,4,5120]{2,1,0:T(4,128)(2,1)} custom-call(bf16[48,640]{1,0:T(8,128)(2,1)S(1)} %get-tuple-element.46.refs_0_, bf16[48,640]{1,0:T(8,128)(2,1)S(1)} %collective-permute-done.14.refs_1_, bf16[96,640]{1,0:T(8,128)(2,1)S(1)} %collective-permute-done.15.refs_2_, bf16[96,640]{1,0:T(8,128)(2,1)S(1)} %collective-permute-done.16.refs_3_, ...), custom_call_target="tpu_custom_call" | custom-call | tf_op jit(solution)/shard_map/pallas_call | solution.py:422
  (60 shorter events, 2.7 us)
Async XLA Ops:
  0.0 15.7 %copy-start = (f32[1,8,320]{2,1,0:T(8,128)S(1)}, f32[1,8,320]{2,1,0:T(8,128)}, u32[]{:S(2)}) copy-start(f32[1,8,320]{2,1,0:T(8,128)} %param.14) | copy-start | bytes 30724
  0.0 5.2 %copy-start.1 = (bf16[192,1,8,320]{3,2,1,0:T(8,128)(2,1)S(1)}, bf16[192,1,8,320]{3,2,1,0:T(8,128)(2,1)}, u32[]{:S(2)}) copy-start(bf16[192,1,8,320]{3,2,1,0:T(8,128)(2,1)} %param.10) | copy-start | bytes 2949124
  2.8 18.0 %collective-permute-start.4 = (bf16[192,640]{1,0:T(8,128)(2,1)}, bf16[192,640]{1,0:T(8,128)(2,1)S(1)}, u32[]{:S(2)}, u32[]{:S(2)}) collective-permute-start(bf16[192,640]{1,0:T(8,128)(2,1)} %get-tuple-element.37), channel_id=1, source_target_pairs={{0,12},{2,14},{4,8},{6,10},{8,4},{10,6},{12,0},{14,2},{1,13},{3,15... | collective-permute-start | bytes 737288 | tf_op jit(solution)/shard_map/ppermute | solution.py:158
  4.1 20.7 %collective-permute-start.3 = (bf16[192,640]{1,0:T(8,128)(2,1)S(1)}, bf16[192,640]{1,0:T(8,128)(2,1)S(1)}, u32[]{:S(2)}, u32[]{:S(2)}) collective-permute-start(bf16[192,640]{1,0:T(8,128)(2,1)S(1)} %get-tuple-element.30.rest_1_), channel_id=1, source_target_pairs={{0,8},{2,10},{4,12},{6,14},{8,0},{10,2},{12,4},{14,6},{1,9},{3,11}... | collective-permute-start | bytes 737288 | tf_op jit(solution)/shard_map/ppermute | solution.py:158
  5.2 1.3 %copy-start.3 = (bf16[192,1,8,320]{3,2,1,0:T(8,128)(2,1)S(1)}, bf16[192,1,8,320]{3,2,1,0:T(8,128)(2,1)}, u32[]{:S(2)}) copy-start(bf16[192,1,8,320]{3,2,1,0:T(8,128)(2,1)} %param.11) | copy-start | bytes 2949124
  6.5 0.7 copy-start.8
  8.9 0.7 copy-start.6
  9.6 7.8 %collective-permute-start = (bf16[192,640]{1,0:T(8,128)(2,1)}, bf16[192,640]{1,0:T(8,128)(2,1)S(1)}, u32[]{:S(2)}, u32[]{:S(2)}) collective-permute-start(bf16[192,640]{1,0:T(8,128)(2,1)} %get-tuple-element.32), channel_id=1, source_target_pairs={{0,2},{2,0},{4,6},{6,4},{8,10},{10,8},{12,14},{14,12},{1,3},{3,1},... | collective-permute-start | bytes 737288 | tf_op jit(solution)/shard_map/ppermute | solution.py:158
  10.7 14.2 %collective-permute-start.1 = (bf16[192,640]{1,0:T(8,128)(2,1)}, bf16[192,640]{1,0:T(8,128)(2,1)S(1)}, u32[]{:S(2)}, u32[]{:S(2)}) collective-permute-start(bf16[192,640]{1,0:T(8,128)(2,1)} %get-tuple-element.35), channel_id=1, source_target_pairs={{0,4},{2,6},{4,0},{6,2},{8,12},{10,14},{12,8},{14,10},{1,5},{3,7},... | collective-permute-start | bytes 737288 | tf_op jit(solution)/shard_map/ppermute | solution.py:158
  11.6 17.0 %collective-permute-start.2 = (bf16[192,640]{1,0:T(8,128)(2,1)}, bf16[192,640]{1,0:T(8,128)(2,1)S(1)}, u32[]{:S(2)}, u32[]{:S(2)}) collective-permute-start(bf16[192,640]{1,0:T(8,128)(2,1)} %get-tuple-element.36), channel_id=1, source_target_pairs={{0,6},{2,4},{4,2},{6,0},{8,14},{10,12},{12,10},{14,8},{1,7},{3,5},... | collective-permute-start | bytes 737288 | tf_op jit(solution)/shard_map/ppermute | solution.py:158
  13.4 1.6 %copy-start.10 = (s32[8]{0:T(128)S(1)}, s32[8]{0:T(128)}, u32[]{:S(2)}) copy-start(s32[8]{0:T(128)} %param.15) | copy-start | bytes 100
  15.7 1.7 %copy-start.7 = (bf16[192,640]{1,0:T(8,128)(2,1)S(1)}, bf16[192,640]{1,0:T(8,128)(2,1)}, u32[]{:S(2)}) copy-start(bf16[192,640]{1,0:T(8,128)(2,1)} %copy-done.6) | copy-start | bytes 737284
  15.7 2.9 %copy-start.5 = (bf16[192,1,8,320]{3,2,1,0:T(8,128)(2,1)S(1)}, bf16[192,1,8,320]{3,2,1,0:T(8,128)(2,1)}, u32[]{:S(2)}) copy-start(bf16[192,1,8,320]{3,2,1,0:T(8,128)(2,1)} %param.9) | copy-start | bytes 2949124
  17.3 1.3 %copy-start.2 = (bf16[192,1,8,320]{3,2,1,0:T(8,128)(2,1)S(1)}, bf16[192,1,8,320]{3,2,1,0:T(8,128)(2,1)}, u32[]{:S(2)}) copy-start(bf16[192,1,8,320]{3,2,1,0:T(8,128)(2,1)} %param.10) | copy-start | bytes 2949124
  17.3 1.7 %copy-start.4 = (bf16[192,1,8,320]{3,2,1,0:T(8,128)(2,1)S(1)}, bf16[192,1,8,320]{3,2,1,0:T(8,128)(2,1)}, u32[]{:S(2)}) copy-start(bf16[192,1,8,320]{3,2,1,0:T(8,128)(2,1)} %param.11) | copy-start | bytes 2949124
  17.3 1.7 %copy-start.9 = (f32[1,8,192]{2,1,0:T(8,128)S(1)}, f32[1,8,192]{2,1,0:T(8,128)}, u32[]{:S(2)}) copy-start(f32[1,8,192]{2,1,0:T(8,128)} %param.12) | copy-start | bytes 18436
  29.9 30.9 %collective-permute-start.13 = (bf16[480,640]{1,0:T(8,128)(2,1)S(1)}, bf16[480,640]{1,0:T(8,128)(2,1)S(1)}, u32[]{:S(2)}, u32[]{:S(2)}) collective-permute-start(bf16[480,640]{1,0:T(8,128)(2,1)S(1)} %shard_map.101.refs_3_), channel_id=1, source_target_pairs={{0,8},{2,10},{4,12},{6,14},{8,0},{10,2},{12,4},{14,6},{1,9},{3,11}... | collective-permute-start | bytes 1843208 | tf_op jit(solution)/shard_map/ppermute | solution.py:158
  33.1 2.0 %collective-permute-start.9 = (bf16[192,640]{1,0:T(8,128)(2,1)S(1)}, bf16[192,640]{1,0:T(8,128)(2,1)S(1)}, u32[]{:S(2)}, u32[]{:S(2)}) collective-permute-start(bf16[192,640]{1,0:T(8,128)(2,1)S(1)} %shard_map.100.refs_6_), channel_id=1, source_target_pairs={{0,2},{2,0},{4,6},{6,4},{8,10},{10,8},{12,14},{14,12},{1,3},{3,1},... | collective-permute-start | bytes 737288 | tf_op jit(solution)/shard_map/ppermute | solution.py:158
  33.8 19.0 %collective-permute-start.6 = (bf16[192,640]{1,0:T(8,128)(2,1)S(1)}, bf16[192,640]{1,0:T(8,128)(2,1)S(1)}, u32[]{:S(2)}, u32[]{:S(2)}) collective-permute-start(bf16[192,640]{1,0:T(8,128)(2,1)S(1)} %shard_map.97.refs_8_), channel_id=1, source_target_pairs={{0,6},{2,4},{4,2},{6,0},{8,14},{10,12},{12,10},{14,8},{1,7},{3,5},... | collective-permute-start | bytes 737288 | tf_op jit(solution)/shard_map/ppermute | solution.py:158
  33.8 22.7 %collective-permute-start.5 = (bf16[192,640]{1,0:T(8,128)(2,1)S(1)}, bf16[192,640]{1,0:T(8,128)(2,1)S(1)}, u32[]{:S(2)}, u32[]{:S(2)}) collective-permute-start(bf16[192,640]{1,0:T(8,128)(2,1)S(1)} %shard_map.96.refs_7_), channel_id=1, source_target_pairs={{0,4},{2,6},{4,0},{6,2},{8,12},{10,14},{12,8},{14,10},{1,5},{3,7},... | collective-permute-start | bytes 737288 | tf_op jit(solution)/shard_map/ppermute | solution.py:158
  36.4 24.4 %collective-permute-start.11 = (bf16[192,640]{1,0:T(8,128)(2,1)S(1)}, bf16[192,640]{1,0:T(8,128)(2,1)S(1)}, u32[]{:S(2)}, u32[]{:S(2)}) collective-permute-start(bf16[192,640]{1,0:T(8,128)(2,1)S(1)} %shard_map.104.refs_2_), channel_id=1, source_target_pairs={{0,2},{2,0},{4,6},{6,4},{8,10},{10,8},{12,14},{14,12},{1,3},{3,1},... | collective-permute-start | bytes 737288 | tf_op jit(solution)/shard_map/ppermute | solution.py:158
  37.2 23.5 %collective-permute-start.12 = (bf16[192,640]{1,0:T(8,128)(2,1)S(1)}, bf16[192,640]{1,0:T(8,128)(2,1)S(1)}, u32[]{:S(2)}, u32[]{:S(2)}) collective-permute-start(bf16[192,640]{1,0:T(8,128)(2,1)S(1)} %shard_map.105.refs_4_), channel_id=1, source_target_pairs={{0,2},{2,0},{4,6},{6,4},{8,10},{10,8},{12,14},{14,12},{1,3},{3,1},... | collective-permute-start | bytes 737288 | tf_op jit(solution)/shard_map/ppermute | solution.py:158
  52.8 3.7 %collective-permute-start.10 = (bf16[96,640]{1,0:T(8,128)(2,1)S(1)}, bf16[96,640]{1,0:T(8,128)(2,1)S(1)}, u32[]{:S(2)}, u32[]{:S(2)}) collective-permute-start(bf16[96,640]{1,0:T(8,128)(2,1)S(1)} %shard_map.103), channel_id=1, source_target_pairs={{0,2},{2,0},{4,6},{6,4},{8,10},{10,8},{12,14},{14,12},{1,3},{3,1},... | collective-permute-start | bytes 368648 | tf_op jit(solution)/shard_map/ppermute | solution.py:158
  56.5 9.2 %collective-permute-start.7 = (bf16[96,640]{1,0:T(8,128)(2,1)S(1)}, bf16[96,640]{1,0:T(8,128)(2,1)S(1)}, u32[]{:S(2)}, u32[]{:S(2)}) collective-permute-start(bf16[96,640]{1,0:T(8,128)(2,1)S(1)} %shard_map.98), channel_id=1, source_target_pairs={{0,4},{2,6},{4,0},{6,2},{8,12},{10,14},{12,8},{14,10},{1,5},{3,7},... | collective-permute-start | bytes 368648 | tf_op jit(solution)/shard_map/ppermute | solution.py:158
  56.5 9.2 %collective-permute-start.8 = (bf16[96,640]{1,0:T(8,128)(2,1)S(1)}, bf16[96,640]{1,0:T(8,128)(2,1)S(1)}, u32[]{:S(2)}, u32[]{:S(2)}) collective-permute-start(bf16[96,640]{1,0:T(8,128)(2,1)S(1)} %shard_map.99), channel_id=1, source_target_pairs={{0,6},{2,4},{4,2},{6,0},{8,14},{10,12},{12,10},{14,8},{1,7},{3,5},... | collective-permute-start | bytes 368648 | tf_op jit(solution)/shard_map/ppermute | solution.py:158
  68.1 7.4 %collective-permute-start.15 = (bf16[96,640]{1,0:T(8,128)(2,1)S(1)}, bf16[96,640]{1,0:T(8,128)(2,1)S(1)}, u32[]{:S(2)}, u32[]{:S(2)}) collective-permute-start(bf16[96,640]{1,0:T(8,128)(2,1)S(1)} %get-tuple-element.48), channel_id=1, source_target_pairs={{0,8},{1,9},{2,10},{3,11},{4,12},{5,13},{6,14},{7,15},{8,0},{9,1},... | collective-permute-start | bytes 368648 | tf_op jit(solution)/shard_map/ppermute | solution.py:149
  69.7 6.9 %collective-permute-start.17 = (bf16[96,640]{1,0:T(8,128)(2,1)S(1)}, bf16[96,640]{1,0:T(8,128)(2,1)S(1)}, u32[]{:S(2)}, u32[]{:S(2)}) collective-permute-start(bf16[96,640]{1,0:T(8,128)(2,1)S(1)} %get-tuple-element.49), channel_id=1, source_target_pairs={{0,1},{1,0},{2,3},{3,2},{4,5},{5,4},{6,7},{7,6},{8,9},{9,8},{10,11... | collective-permute-start | bytes 368648 | tf_op jit(solution)/shard_map/ppermute | solution.py:149
  70.9 6.8 %collective-permute-start.19 = (bf16[96,640]{1,0:T(8,128)(2,1)S(1)}, bf16[96,640]{1,0:T(8,128)(2,1)S(1)}, u32[]{:S(2)}, u32[]{:S(2)}) collective-permute-start(bf16[96,640]{1,0:T(8,128)(2,1)S(1)} %get-tuple-element.50), channel_id=1, source_target_pairs={{0,4},{1,5},{2,6},{3,7},{4,0},{5,1},{6,2},{7,3},{8,12},{9,13},{10,... | collective-permute-start | bytes 368648 | tf_op jit(solution)/shard_map/ppermute | solution.py:149
  71.5 9.3 %collective-permute-start.21 = (bf16[96,640]{1,0:T(8,128)(2,1)S(1)}, bf16[96,640]{1,0:T(8,128)(2,1)S(1)}, u32[]{:S(2)}, u32[]{:S(2)}) collective-permute-start(bf16[96,640]{1,0:T(8,128)(2,1)S(1)} %get-tuple-element.51), channel_id=1, source_target_pairs={{0,5},{1,4},{2,7},{3,6},{4,1},{5,0},{6,3},{7,2},{8,13},{9,12},{10,... | collective-permute-start | bytes 368648 | tf_op jit(solution)/shard_map/ppermute | solution.py:149
  72.3 2.4 %collective-permute-start.14 = (bf16[48,640]{1,0:T(8,128)(2,1)S(1)}, bf16[48,640]{1,0:T(8,128)(2,1)S(1)}, u32[]{:S(2)}, u32[]{:S(2)}) collective-permute-start(bf16[48,640]{1,0:T(8,128)(2,1)S(1)} %get-tuple-element.47), channel_id=1, source_target_pairs={{0,2},{2,0},{4,6},{6,4},{8,10},{10,8},{12,14},{14,12},{1,3},{3,1},... | collective-permute-start | bytes 184328 | tf_op jit(solution)/shard_map/ppermute | solution.py:158
  74.7 8.3 %collective-permute-start.23 = (bf16[96,640]{1,0:T(8,128)(2,1)S(1)}, bf16[96,640]{1,0:T(8,128)(2,1)S(1)}, u32[]{:S(2)}, u32[]{:S(2)}) collective-permute-start(bf16[96,640]{1,0:T(8,128)(2,1)S(1)} %get-tuple-element.52), channel_id=1, source_target_pairs={{0,9},{1,8},{2,11},{3,10},{4,13},{5,12},{6,15},{7,14},{8,1},{9,0},... | collective-permute-start | bytes 368648 | tf_op jit(solution)/shard_map/ppermute | solution.py:149
  75.5 14.8 %collective-permute-start.25 = (bf16[96,640]{1,0:T(8,128)(2,1)S(1)}, bf16[96,640]{1,0:T(8,128)(2,1)S(1)}, u32[]{:S(2)}, u32[]{:S(2)}) collective-permute-start(bf16[96,640]{1,0:T(8,128)(2,1)S(1)} %get-tuple-element.53), channel_id=1, source_target_pairs={{0,12},{1,13},{2,14},{3,15},{4,8},{5,9},{6,10},{7,11},{8,4},{9,5},... | collective-permute-start | bytes 368648 | tf_op jit(solution)/shard_map/ppermute | solution.py:149
  76.6 16.2 %collective-permute-start.27 = (bf16[96,640]{1,0:T(8,128)(2,1)S(1)}, bf16[96,640]{1,0:T(8,128)(2,1)S(1)}, u32[]{:S(2)}, u32[]{:S(2)}) collective-permute-start(bf16[96,640]{1,0:T(8,128)(2,1)S(1)} %get-tuple-element.54), channel_id=1, source_target_pairs={{0,13},{1,12},{2,15},{3,14},{4,9},{5,8},{6,11},{7,10},{8,5},{9,4},... | collective-permute-start | bytes 368648 | tf_op jit(solution)/shard_map/ppermute | solution.py:149
  77.7 16.3 %collective-permute-start.16 = (bf16[96,640]{1,0:T(8,128)(2,1)S(1)}, bf16[96,640]{1,0:T(8,128)(2,1)S(1)}, u32[]{:S(2)}, u32[]{:S(2)}) collective-permute-start(bf16[96,640]{1,0:T(8,128)(2,1)S(1)} %collective-permute-done.15.refs_2_), channel_id=1, source_target_pairs={{0,2},{2,0},{4,6},{6,4},{8,10},{10,8},{12,14},{14,12},{1,3},{3,1},... | collective-permute-start | bytes 368648 | tf_op jit(solution)/shard_map/ppermute | solution.py:158
  80.8 13.2 %collective-permute-start.18 = (bf16[96,640]{1,0:T(8,128)(2,1)S(1)}, bf16[96,640]{1,0:T(8,128)(2,1)S(1)}, u32[]{:S(2)}, u32[]{:S(2)}) collective-permute-start(bf16[96,640]{1,0:T(8,128)(2,1)S(1)} %collective-permute-done.17.refs_4_), channel_id=1, source_target_pairs={{0,2},{2,0},{4,6},{6,4},{8,10},{10,8},{12,14},{14,12},{1,3},{3,1},... | collective-permute-start | bytes 368648 | tf_op jit(solution)/shard_map/ppermute | solution.py:158
  83.0 11.5 %collective-permute-start.20 = (bf16[96,640]{1,0:T(8,128)(2,1)S(1)}, bf16[96,640]{1,0:T(8,128)(2,1)S(1)}, u32[]{:S(2)}, u32[]{:S(2)}) collective-permute-start(bf16[96,640]{1,0:T(8,128)(2,1)S(1)} %collective-permute-done.19.refs_6_), channel_id=1, source_target_pairs={{0,2},{2,0},{4,6},{6,4},{8,10},{10,8},{12,14},{14,12},{1,3},{3,1},... | collective-permute-start | bytes 368648 | tf_op jit(solution)/shard_map/ppermute | solution.py:158
  90.3 4.2 %collective-permute-start.22 = (bf16[96,640]{1,0:T(8,128)(2,1)S(1)}, bf16[96,640]{1,0:T(8,128)(2,1)S(1)}, u32[]{:S(2)}, u32[]{:S(2)}) collective-permute-start(bf16[96,640]{1,0:T(8,128)(2,1)S(1)} %collective-permute-done.21.refs_8_), channel_id=1, source_target_pairs={{0,2},{2,0},{4,6},{6,4},{8,10},{10,8},{12,14},{14,12},{1,3},{3,1},... | collective-permute-start | bytes 368648 | tf_op jit(solution)/shard_map/ppermute | solution.py:158
  92.8 2.2 %collective-permute-start.24 = (bf16[96,640]{1,0:T(8,128)(2,1)S(1)}, bf16[96,640]{1,0:T(8,128)(2,1)S(1)}, u32[]{:S(2)}, u32[]{:S(2)}) collective-permute-start(bf16[96,640]{1,0:T(8,128)(2,1)S(1)} %collective-permute-done.23.refs_10_), channel_id=1, source_target_pairs={{0,2},{2,0},{4,6},{6,4},{8,10},{10,8},{12,14},{14,12},{1,3},{3,1},... | collective-permute-start | bytes 368648 | tf_op jit(solution)/shard_map/ppermute | solution.py:158
  94.0 1.3 %collective-permute-start.26 = (bf16[96,640]{1,0:T(8,128)(2,1)S(1)}, bf16[96,640]{1,0:T(8,128)(2,1)S(1)}, u32[]{:S(2)}, u32[]{:S(2)}) collective-permute-start(bf16[96,640]{1,0:T(8,128)(2,1)S(1)} %collective-permute-done.25.refs_12_), channel_id=1, source_target_pairs={{0,2},{2,0},{4,6},{6,4},{8,10},{10,8},{12,14},{14,12},{1,3},{3,1},... | collective-permute-start | bytes 368648 | tf_op jit(solution)/shard_map/ppermute | solution.py:158
  94.0 1.5 %collective-permute-start.28 = (bf16[96,640]{1,0:T(8,128)(2,1)S(1)}, bf16[96,640]{1,0:T(8,128)(2,1)S(1)}, u32[]{:S(2)}, u32[]{:S(2)}) collective-permute-start(bf16[96,640]{1,0:T(8,128)(2,1)S(1)} %collective-permute-done.27.refs_14_), channel_id=1, source_target_pairs={{0,2},{2,0},{4,6},{6,4},{8,10},{10,8},{12,14},{14,12},{1,3},{3,1},... | collective-permute-start | bytes 368648 | tf_op jit(solution)/shard_map/ppermute | solution.py:158
